TPU v7x, 256 devices: a whole 4x4x8 slice. The times are simulated.
256 devices in a mesh: ctx: 16 (over z, core), exp: 16 (over x, y).
Axes of the slice: x: 4, y: 4, z: 8, core: 2. Of those that a mesh axis runs over, the one named last changes fastest.
Arguments:
- queries: bfloat16 [2048, 4096], P('exp'), may hold values from -16 to 16
- cache_kv: bfloat16 [2, 64, 4096, 512], P(None, 'exp', 'ctx'), may hold values from -16 to 16
- block_kv: bfloat16 [2, 64, 32, 512], P(None, 'exp', 'ctx'), may hold values from -6 to 6
- stream_in: bfloat16 [2048, 4096], P('exp'), may hold values from -6 to 6
- out_proj: bfloat16 [4096, 4096], P('ctx'), may hold values from -0.25 to 0.25
- norm_gain: float32 [4096], replicated, may hold values from 0.1 to 1.9
- expert_ids: int32 [2048, 8], P('exp'), may hold values from 0 to 127, all different within a row; in each aligned block of 128 rows (0 to 127, 128 to 255, ...) at most 16 rows name the same one
- gate_weights: float32 [2048, 8], P('exp'), may hold values from 0.03 to 0.3
- expert_in: bfloat16 [2, 16, 4096, 4096], P(None, 'exp', None, 'ctx'), may hold values from -0.09375 to 0.09375
- expert_out: bfloat16 [16, 4096, 4096], P('exp', 'ctx'), may hold values from -0.375 to 0.375
Outputs:
- mixed_out: bfloat16 [2048, 4096], P('exp', 'ctx')
Inputs may be any that keep to these rules, and one draw needn't show every extreme that they name: `expert_ids`: each row names 8 different experts; in each aligned block of 128 rows (the rows of one index of exp) no expert is named by more than 16 rows, a bound that some block reaches.
All inputs are finite; a program needn't handle non-finite values.
Results may differ from a plain program's by a relative error of at most 0.035.
Values may be sent and summed in bfloat16 or wider, within the bound.
A program may use at most 192 MiB of HBM per device.

v0:
```python
import jax
import jax.numpy as jnp
from jax import lax
from jax.sharding import PartitionSpec as P

D = 4096
H = 32
KVH = 4
HD = 128
TOP = 8
SPLIT = 2


def body(
    queries,
    cache_kv,
    block_kv,
    stream_in,
    out_proj,
    norm_gain,
    expert_ids,
    gate_weights,
    expert_in,
    expert_out,
):
    ctx_size = lax.axis_size("ctx")
    exp_size = lax.axis_size("exp")
    group = H // KVH
    seq_count = cache_kv.shape[1]
    rows_g = queries.shape[0]
    masked_rows = rows_g // seq_count
    query_heads = queries.reshape(seq_count, masked_rows, KVH, group, HD)
    cache_keys = cache_kv[0].reshape(seq_count, -1, KVH, HD)
    cache_values = cache_kv[1].reshape(seq_count, -1, KVH, HD)
    block_keys = block_kv[0].reshape(seq_count, -1, KVH, HD)
    block_values = block_kv[1].reshape(seq_count, -1, KVH, HD)
    factor_scale = HD ** (-0.5)
    prompt_scores = (
        jnp.einsum("smkgd,snkd->smkgn", query_heads, cache_keys, preferred_element_type=jnp.float32)
        * factor_scale
    )
    block_scores = (
        jnp.einsum("smkgd,snkd->smkgn", query_heads, block_keys, preferred_element_type=jnp.float32)
        * factor_scale
    )
    scores = jnp.concatenate([prompt_scores, block_scores], axis=-1)
    row_peak = jnp.max(scores, axis=-1)
    weights = jnp.exp(scores - row_peak[..., None])
    row_total = jnp.sum(weights, axis=-1)
    rounded = weights.astype(jnp.bfloat16)
    prompt_width = cache_keys.shape[1]
    weighted = jnp.einsum(
        "smkgn,snkd->smkgd",
        rounded[..., :prompt_width],
        cache_values,
        preferred_element_type=jnp.float32,
    )
    weighted = weighted + jnp.einsum(
        "smkgn,snkd->smkgd",
        rounded[..., prompt_width:],
        block_values,
        preferred_element_type=jnp.float32,
    )
    heads_here = H // ctx_size
    peaks_in, totals_in, values_in = (
        lax.all_to_all(
            row_peak.reshape(1, rows_g, H), "ctx", split_axis=2, concat_axis=0, tiled=True
        ),
        lax.all_to_all(
            row_total.reshape(1, rows_g, H), "ctx", split_axis=2, concat_axis=0, tiled=True
        ),
        lax.all_to_all(
            weighted.reshape(1, rows_g, H, HD), "ctx", split_axis=2, concat_axis=0, tiled=True
        ),
    )
    top_peak = jnp.max(peaks_in, axis=0)
    source_factor = jnp.exp(peaks_in - top_peak[None])
    total_here = jnp.sum(totals_in * source_factor, axis=0)
    values_here = jnp.sum(values_in * source_factor[..., None], axis=0)
    attended = (values_here / total_here[..., None]).astype(jnp.bfloat16)
    projected = jnp.dot(
        attended.reshape(rows_g, heads_here * HD), out_proj, preferred_element_type=jnp.float32
    )
    col_width = D // ctx_size
    col_start = lax.axis_index("ctx") * col_width
    proj_whole = lax.psum(projected.astype(jnp.bfloat16), "ctx").astype(jnp.float32)
    stream = (stream_in.astype(jnp.float32) + proj_whole).astype(jnp.bfloat16)
    widened = stream.astype(jnp.float32)
    inverse = lax.rsqrt(jnp.mean(widened * widened, axis=1, keepdims=True) + 1e-06)
    normed = (widened * inverse * norm_gain[None, :]).astype(jnp.bfloat16)
    stream_cols = lax.dynamic_slice_in_dim(stream, col_start, col_width, 1)
    owned_here = ctx_size // SPLIT
    experts_all = exp_size * owned_here
    capacity = (2 * rows_g * TOP + experts_all - 1) // experts_all
    flat_ids = expert_ids.reshape(-1)
    chosen_pick = flat_ids % owned_here == lax.axis_index("ctx") // SPLIT
    owner_exp = flat_ids // owned_here
    owner_hit = jnp.where(
        chosen_pick[:, None]
        & (owner_exp[:, None] == jnp.arange(exp_size, dtype=jnp.int32)[None, :]),
        1,
        0,
    )
    before_here = jnp.cumsum(owner_hit, axis=0) - owner_hit
    slot_rank = jnp.sum(before_here * owner_hit, axis=1)
    target_slot = owner_exp * capacity + slot_rank
    slot_hit = chosen_pick[:, None] & (
        target_slot[:, None] == jnp.arange(exp_size * capacity, dtype=jnp.int32)[None, :]
    )
    slot_hit = slot_hit.reshape(rows_g, TOP, exp_size * capacity)
    placement_map = jnp.sum(slot_hit.astype(jnp.float32), axis=1).astype(jnp.bfloat16)
    combine_weights = jnp.sum(jnp.where(slot_hit, gate_weights[:, :, None], 0.0), axis=1)
    outgoing = jnp.einsum(
        "rs,rd->sd", placement_map, normed, preferred_element_type=jnp.float32
    ).astype(jnp.bfloat16)
    outgoing = outgoing.reshape(exp_size, capacity, D)
    gate_up = expert_in[:, 0]
    w_down = expert_out[0]
    arrived = lax.all_to_all(outgoing, "exp", split_axis=0, concat_axis=0, tiled=True)
    flat_rows = arrived.reshape(-1, D)
    both_parts = jnp.einsum("rd,cdh->crh", flat_rows, gate_up, preferred_element_type=jnp.float32)
    hidden_act = (jax.nn.silu(both_parts[0]) * both_parts[1]).astype(jnp.bfloat16)
    result = jnp.dot(hidden_act, w_down, preferred_element_type=jnp.float32)
    result = result.reshape(arrived.shape[0], arrived.shape[1], D)
    returned_rows = lax.all_to_all(
        result.astype(jnp.bfloat16), "exp", split_axis=0, concat_axis=0, tiled=True
    ).astype(result.dtype)
    expert_part = jnp.dot(
        combine_weights,
        returned_rows.reshape(exp_size * capacity, D),
        precision=lax.Precision.HIGHEST,
        preferred_element_type=jnp.float32,
    )
    expert_cols = lax.psum_scatter(
        expert_part.astype(jnp.bfloat16), "ctx", scatter_dimension=1, tiled=True
    ).astype(jnp.float32)
    return (stream_cols.astype(jnp.float32) + expert_cols).astype(jnp.bfloat16)


def solution(mesh):
    placed = (
        P("exp", None),
        P(None, "exp", "ctx", None),
        P(None, "exp", "ctx", None),
        P("exp", None),
        P("ctx", None),
        P(),
        P("exp", None),
        P("exp", None),
        P(None, "exp", None, "ctx"),
        P("exp", "ctx", None),
    )
    return jax.shard_map(
        body, mesh=mesh, in_specs=placed, out_specs=P("exp", "ctx"), check_vma=False
    )
```

profile of v0, /device:TPU:1, one launch (start us, length us, event | category | flops | bytes accessed | tf_op | source)
XLA Modules:
  0.0 356.8 jit_solution(4741986209521739916)
XLA Ops:
  6.5 1.6 copy.179
  8.2 1.5 fusion.19
  9.7 1.6 fusion.45
  11.3 2.3 copy.177
  13.5 3.9 %fusion.46 = (f32[4,32,4,8]{1,3,2,0:T(8,128)S(1)}, f32[4,32,4,8,256]{4,1,3,2,0:T(8,128)}) fusion(bf16[4,256,4,128,1]{1,3,4,2,0:T(8,128)(2,1)} %bitcast.100, bf16[4,32,4,8,128]{4,3,2,1,0:T(8,128)(2,1)S(1)} %bitcast.95), kind=kOutput, calls=%fused_computation.87 | convolution fusion | flops 270528512 | bytes 6307840 | tf_op jit(solution)/shard_map/smkgd,snkd->smkgn/dot_general | solution.py:39
  17.5 0.7 reduce_max.43
  18.2 10.0 %all-to-all-start.1 = ((f32[1,128,32]{1,0,2:T(1,128)}), f32[1,128,32]{1,0,2:T(1,128)S(1)}, u32[]{:S(2)}, u32[]{:S(2)}) async-start(f32[1,128,32]{1,0,2:T(1,128)} %bitcast.17), calls=%async_computation.1 | async-start | bytes 32768 | tf_op jit(solution)/shard_map/all_to_all | solution.py:66
  28.2 2.2 copy.146
  30.4 1.5 copy.178
  31.9 3.7 %fusion.1 = (f32[4,32,4,8]{1,3,2,0:T(8,128)S(1)}, bf16[4,32,4,8,258]{4,1,3,2,0:T(8,128)(2,1)S(1)}) fusion(f32[4,32,4,8,2]{4,1,3,2,0:T(8,128)} %copy.146, f32[4,32,4,8,256]{4,1,3,2,0:T(8,128)} %get-tuple-element.16, f32[4,32,4,8]{1,3,2,0:T(8,128)S(1)} %reduce_max.42), kind=kLoop, calls=%fused_computation.6 | loop fusion | flops 4222976 | bytes 6373376 | tf_op jit(solution)/shard_map/reduce_sum | solution.py:49
  35.9 2.7 fusion.9
  38.9 0.7 reshape.181
  39.6 7.2 %all-to-all-start.2 = ((f32[1,128,32]{1,0,2:T(1,128)}), f32[1,128,32]{1,0,2:T(1,128)S(1)}, u32[]{:S(2)}, u32[]{:S(2)}) async-start(f32[1,128,32]{1,0,2:T(1,128)} %bitcast.22), calls=%async_computation.2 | async-start | bytes 32768 | tf_op jit(solution)/shard_map/all_to_all | solution.py:69
  46.8 2.1 add_bitcast_fusion
  49.2 2.5 copy.153
  51.7 2.4 all-to-all-done.2
  54.2 4.9 %all-to-all-start = ((f32[1,128,32,128]{3,1,0,2:T(8,128)}), f32[1,128,32,128]{3,1,0,2:T(8,128)}, u32[]{:S(2)}, u32[]{:S(2)}) async-start(f32[1,128,32,128]{3,1,0,2:T(8,128)} %copy.153), calls=%async_computation | async-start | bytes 4194304 | tf_op jit(solution)/shard_map/all_to_all | solution.py:72
  59.5 4.5 %reduce-window.6 = s32[16,8,128]{2,1,0:T(8,128)S(1)} reduce-window(s32[16,8,128]{2,1,0:T(8,128)S(1)} %fusion.31, s32[]{:T(128)} %constant.56.clone.1), window={size=1x1x128 pad=0_0x0_0x127_0}, to_apply=%region_7.8 | reduce-window | flops 2080768 | bytes 131076 | tf_op jit(solution)/shard_map/reduce-window
  64.6 43.6 %all-to-all-done = f32[1,128,32,128]{3,1,0,2:T(8,128)} async-done(((f32[1,128,32,128]{3,1,0,2:T(8,128)}), f32[1,128,32,128]{3,1,0,2:T(8,128)}, u32[]{:S(2)}, u32[]{:S(2)}) %all-to-all-start) | async-done | bytes 2097184 | tf_op jit(solution)/shard_map/all_to_all | solution.py:72
  108.1 1.9 multiply_reduce_fusion
  110.3 3.1 convolution_convert_fusion.3
  114.0 0.9 convert_reduce_fusion
  114.9 108.9 %all-reduce.2.cloned.1.call-done = bf16[128,4096]{1,0:T(8,128)(2,1)} async-done(((bf16[128,4096]{1,0:T(8,128)(2,1)}), bf16[128,4096]{1,0:T(8,128)(2,1)}) %all-reduce.2.cloned.1.call-update) | async-done | bytes 1048592 | tf_op jit(solution)/shard_map/psum | solution.py:86
  223.8 2.0 fusion.5
  225.8 0.8 convolution_convert_fusion
  226.6 33.7 %all_to_all.64 = bf16[16,16,4096]{2,1,0:T(8,128)(2,1)S(1)} all-to-all(bf16[16,16,4096]{2,1,0:T(8,128)(2,1)S(1)} %bitcast.97), channel_id=1, replica_groups=mesh['ctx'=16,'exp'=16] {'exp'}, dimensions={0} | all-to-all | bytes 4194304 | tf_op jit(solution)/shard_map/all_to_all | solution.py:119
  260.3 1.2 fusion.11
  261.7 0.7 convolution_convert_fusion.1
  262.4 29.4 %all_to_all.65 = bf16[16,16,4096]{2,1,0:T(8,128)(2,1)S(1)} all-to-all(bf16[16,16,4096]{2,1,0:T(8,128)(2,1)S(1)} %convolution_convert_fusion.1), channel_id=1, replica_groups=mesh['ctx'=16,'exp'=16] {'exp'}, dimensions={0} | all-to-all | bytes 4194304 | tf_op jit(solution)/shard_map/all_to_all | solution.py:125
  291.8 2.0 convolution_convert_fusion.2
  293.8 54.7 %reduce-scatter.2.cloned.1.call-done = bf16[128,256]{1,0:T(8,128)(2,1)} async-done(((bf16[128,4096]{1,0:T(8,128)(2,1)}), bf16[128,256]{1,0:T(8,128)(2,1)}) %reduce-scatter.2.cloned.1.call-update) | async-done | bytes 65552 | tf_op jit(solution)/shard_map/reduce_scatter | solution.py:134
  348.5 1.5 add_convert_fusion.1
  (52 shorter events, 2.6 us)
Async XLA Ops:
  6.5 255.1 %copy-start = (bf16[1,256,4096]{2,1,0:T(8,128)(2,1)S(1)}, bf16[1,256,4096]{2,1,0:T(8,128)(2,1)}, u32[]{:S(2)}) copy-start(bf16[1,256,4096]{2,1,0:T(8,128)(2,1)} %param.19) | copy-start | bytes 6291460
  6.5 1.6 copy-start.2
  6.5 3.1 copy-start.1
  18.2 21.4 %all-to-all-start.1 = ((f32[1,128,32]{1,0,2:T(1,128)}), f32[1,128,32]{1,0,2:T(1,128)S(1)}, u32[]{:S(2)}, u32[]{:S(2)}) async-start(f32[1,128,32]{1,0,2:T(1,128)} %bitcast.17), calls=%async_computation.1 | async-start | bytes 32768 | tf_op jit(solution)/shard_map/all_to_all | solution.py:66
  39.6 14.6 %all-to-all-start.2 = ((f32[1,128,32]{1,0,2:T(1,128)}), f32[1,128,32]{1,0,2:T(1,128)S(1)}, u32[]{:S(2)}, u32[]{:S(2)}) async-start(f32[1,128,32]{1,0,2:T(1,128)} %bitcast.22), calls=%async_computation.2 | async-start | bytes 32768 | tf_op jit(solution)/shard_map/all_to_all | solution.py:69
  51.7 7.4 %copy-start.4 = (s32[128,8]{0,1:T(8,128)S(1)}, s32[128,8]{0,1:T(8,128)}, u32[]{:S(2)}) copy-start(s32[128,8]{0,1:T(8,128)} %param.16) | copy-start | bytes 12292
  54.2 54.0 %all-to-all-start = ((f32[1,128,32,128]{3,1,0,2:T(8,128)}), f32[1,128,32,128]{3,1,0,2:T(8,128)}, u32[]{:S(2)}, u32[]{:S(2)}) async-start(f32[1,128,32,128]{3,1,0,2:T(8,128)} %copy.153), calls=%async_computation | async-start | bytes 4194304 | tf_op jit(solution)/shard_map/all_to_all | solution.py:72
  59.1 164.7 %all-reduce.2.cloned.1.call-start = ((), (), s32[]{:S(2)}) async-start(), calls=%async_computation.6 | async-start | bytes 2097152 | tf_op jit(solution)/shard_map/psum | solution.py:86
  110.3 3.5 copy-start.5
  113.5 112.3 %copy-start.3 = (f32[4096]{0:T(1024)S(1)}, f32[4096]{0:T(1024)}, u32[]{:S(2)}) copy-start(f32[4096]{0:T(1024)} %param.15) | copy-start | bytes 49156
  113.5 235.0 %reduce-scatter.2.cloned.1.call-start = ((), (), s32[]{:S(2)}) async-start(), calls=%async_computation.7 | async-start | bytes 1114112 | tf_op jit(solution)/shard_map/reduce_scatter | solution.py:134
  226.6 33.7 %copy-start.6 = (bf16[2,1,4096,256]{3,2,1,0:T(8,128)(2,1)S(1)}, bf16[2,1,4096,256]{3,2,1,0:T(8,128)(2,1)}, u32[]{:S(2)}) copy-start(bf16[2,1,4096,256]{3,2,1,0:T(8,128)(2,1)} %param.18) | copy-start | bytes 12582916
Sparse Core Ops, SparseCore 0:
  113.6 110.1 all-reduce.1
  293.9 54.5 reduce-scatter.1
where the time goes:
time: 359 us; the launch traced here: 357 us
  waiting for transfers between devices  210 us (58%)
  blocking collectives  63.1 us (18%)
  starting transfers between devices  22.4 us (6%)
  matrix products  18.1 us (5%)
  other arithmetic  15.2 us (4%)
  local copies, waits for them, and re-layouts  14.7 us (4%)
  between operations  13.7 us (4%)
    psum x1, waiting for transfers between devices, body(): lax.psum(projected.astype(jnp.bfloat16), 'ctx').astype(jnp.float32)  109 us
    reduce_scatter x1, waiting for transfers between devices, body(): lax.psum_scatter(expert_part.astype(jnp.bfloat16), 'ctx', scatter_dimensi...  54.7 us
    all_to_all x1, waiting for transfers between devices, body(): lax.all_to_all(weighted.reshape(1, rows_g, H, HD), 'ctx', split_axis=2, c...  43.6 us
    all_to_all x1, blocking collectives, body(): lax.all_to_all(outgoing, 'exp', split_axis=0, concat_axis=0, tiled=True)  33.7 us
    all_to_all x1, blocking collectives, body(): lax.all_to_all(result.astype(jnp.bfloat16), 'exp', split_axis=0, concat_a...  29.4 us
    all_to_all x1, starting transfers between devices, body(): lax.all_to_all(row_peak.reshape(1, rows_g, H), 'ctx', split_axis=2, conca...  9.98 us
    all_to_all x1, starting transfers between devices, body(): lax.all_to_all(row_total.reshape(1, rows_g, H), 'ctx', split_axis=2, conc...  7.23 us
  transfers between devices with their start and end apart: 5, of which 4 were waited for; matrix products, arithmetic and copies ran while one was open for 6% of the time, Pallas kernels for 0%

commit v1 on v0

v1 whole, which is shorter than its diff:
```python
import functools
import math

import jax
import jax.numpy as jnp
from jax import lax
from jax.experimental import pallas as pl
from jax.experimental.pallas import tpu as pltpu
from jax.sharding import PartitionSpec as P

HD = 128
SLOTS = 16
MESH = pl.DeviceIdType.MESH
F32 = jnp.float32
BF16 = jnp.bfloat16
VMEM_LIMIT = 60 * 1024 * 1024


def dot(a, b):
    return jnp.dot(a, b, preferred_element_type=F32)


def remote(src, dst, send_sem, recv_sem, **where):
    return pltpu.make_async_remote_copy(
        src_ref=src,
        dst_ref=dst,
        send_sem=send_sem,
        recv_sem=recv_sem,
        device_id=where,
        device_id_type=MESH,
    )


def wait_for(ref, sem):
    pltpu.make_async_copy(ref, ref, sem).wait()


def blk(index, size):
    return pl.ds(pl.multiple_of(index * size, size), size)


def nearest(step, here, count):
    odd = step % 2
    return (here + odd * ((step + 1) // 2) + (1 - odd) * (count - step // 2)) % count


def attention_kernel(
    dims,
    q_hbm,
    cache_hbm,
    block_ref,
    stream_hbm,
    proj_hbm,
    out_ref,
    q,
    kv,
    sin,
    wo,
    wo_pair,
    stat,
    stat_pair,
    own_o,
    pair_out,
    pair_in,
    z_out,
    z_in,
    zs_out,
    zs_in,
    att,
    att_pair,
    c_out,
    c_in,
    load_sem,
    wo_load,
    wo_send,
    wo_recv,
    stat_send,
    stat_recv,
    pair_send,
    pair_recv,
    z_send,
    z_recv,
    zs_send,
    zs_recv,
    att_send,
    att_recv,
    c_send,
    c_recv,
):
    nz, ng, seqs, masked, group, cw = dims
    ctx = lax.axis_index("ctx")
    z, core = ctx // 2, ctx % 2
    pair = 2 * z + 1 - core
    rows = seqs * masked
    factor = HD**-0.5 * math.log2(math.e)

    loads = [
        pltpu.make_async_copy(q_hbm, q, load_sem.at[0]),
        pltpu.make_async_copy(cache_hbm, kv, load_sem.at[1]),
        pltpu.make_async_copy(stream_hbm.at[:, blk(ctx, cw)], sin, load_sem.at[2]),
    ]
    for copy in loads:
        copy.start()
    for b in range(nz):
        pltpu.make_async_copy(
            proj_hbm.at[:, blk(2 * b + core, cw)], wo.at[b], wo_load
        ).start()

    barrier = pltpu.get_barrier_semaphore()
    pl.semaphore_signal(barrier, inc=1, device_id={"ctx": pair}, device_id_type=MESH)
    for t in range(1, nz):
        there = 2 * ((z + t) % nz) + core
        pl.semaphore_signal(barrier, inc=1, device_id={"ctx": there}, device_id_type=MESH)
    pl.semaphore_wait(barrier, nz)

    for b in range(nz):
        remote(
            proj_hbm.at[:, blk(2 * b + 1 - core, cw)], wo_pair.at[b], wo_send, wo_recv, ctx=pair
        ).start()

    for copy in loads:
        copy.wait()

    lane = lax.broadcasted_iota(jnp.int32, (masked, 128), 1)

    def attend(i):
        j = (z // 2 + i) % ng
        for s in range(seqs):
            here = pl.ds(s * masked, masked)
            keys = kv[0, s, :, blk(j, HD)]
            values = kv[1, s, :, blk(j, HD)]
            block_keys = block_ref[0, s, :, blk(j, HD)].astype(F32)
            block_values = block_ref[1, s, :, blk(j, HD)].astype(F32)
            heads = []
            for side in range(2):
                part = core + side - 2 * core * side
                for n in range(group // 2):
                    heads.append(j * group + (n // 2) * 4 + 2 * part + n % 2)
            qs = jnp.concatenate([q[here, blk(h, HD)] for h in heads], axis=0)
            scores = (
                lax.dot_general(
                    qs, keys, (((1,), (1,)), ((), ())), preferred_element_type=F32
                )
                * factor
            )
            qf = qs.astype(F32)
            peak = jnp.max(scores, axis=1, keepdims=True)
            extra = []
            for n in range(block_keys.shape[0]):
                e = jnp.sum(qf * block_keys[n : n + 1], axis=1, keepdims=True) * factor
                extra.append(e)
                peak = jnp.maximum(peak, e)
            weights = jnp.exp2(scores - peak)
            total = jnp.sum(weights, axis=1, keepdims=True)
            summed = dot(weights.astype(BF16), values)
            for n in range(block_keys.shape[0]):
                w = jnp.exp2(extra[n] - peak)
                total = total + w
                summed = summed + w.astype(BF16).astype(F32) * block_values[n : n + 1]
            stats = jnp.zeros((masked, 128), F32)
            for n in range(group):
                side, zz, h = n // 4, (n % 4) // 2, n % 2
                cut = slice(n * masked, (n + 1) * masked)
                at = side * 16 + zz * 8 + h
                stats = jnp.where(lane == at, peak[cut], stats)
                stats = jnp.where(lane == at + 2, total[cut], stats)
                place = pl.ds((n % 4) * HD, HD)
                if side == 0:
                    own_o[i, here, place] = summed[cut]
                else:
                    pair_out[i, here, place] = summed[cut].astype(BF16)
            stat[i, here, :] = stats
        remote(
            pair_out.at[i], pair_in.at[i], pair_send.at[i], pair_recv.at[i], ctx=pair
        ).start()
        remote(
            stat.at[i], stat_pair.at[i], stat_send.at[i], stat_recv.at[i], ctx=pair
        ).start()

    lane_all = lax.broadcasted_iota(jnp.int32, (rows, 128), 1)

    def merge(i):
        j = (z // 2 + i) % ng
        wait_for(pair_in.at[i], pair_recv.at[i])
        wait_for(stat_pair.at[i], stat_recv.at[i])
        mine, theirs = stat[i], stat_pair[i]
        merged = jnp.zeros((rows, 128), F32)
        for zz in range(2):
            for h in range(2):
                at = zz * 8 + h
                m0, m1 = mine[:, at : at + 1], theirs[:, at + 16 : at + 17]
                l0, l1 = mine[:, at + 2 : at + 3], theirs[:, at + 18 : at + 19]
                peak = jnp.maximum(m0, m1)
                f0, f1 = jnp.exp2(m0 - peak), jnp.exp2(m1 - peak)
                merged = jnp.where(lane_all == at, peak, merged)
                merged = jnp.where(lane_all == at + 2, l0 * f0 + l1 * f1, merged)
                place = pl.ds((zz * 2 + h) * HD, HD)
                both = own_o[i, :, place] * f0 + pair_in[i, :, place].astype(F32) * f1
                z_out[2 * j + zz, :, pl.ds(h * HD, HD)] = both.astype(BF16)
        turned = merged.T
        for zz in range(2):
            there = 2 * j + zz
            zs_out[there] = turned[zz * 8 : zz * 8 + 8]

            @pl.when(there == z)
            def _():
                z_in[there] = z_out[there]
                zs_in[there] = zs_out[there]

            @pl.when(there != z)
            def _():
                remote(
                    z_out.at[there],
                    z_in.at[z],
                    z_send.at[there],
                    z_recv.at[z],
                    ctx=2 * there + core,
                ).start()
                remote(
                    zs_out.at[there],
                    zs_in.at[z],
                    zs_send.at[there],
                    zs_recv.at[z],
                    ctx=2 * there + core,
                ).start()

    attend(0)

    def turn(i, carry):
        attend(i)
        merge(i - 1)
        return carry

    lax.fori_loop(1, ng, turn, 0)
    merge(ng - 1)

    for t in range(1, nz):
        source = (z + t) % nz
        wait_for(z_in.at[source], z_recv.at[source])
        wait_for(zs_in.at[source], zs_recv.at[source])
    turned = jnp.concatenate([zs_in[b] for b in range(nz)], axis=0).T
    for h in range(2):
        peaks = [turned[:, 8 * b + h : 8 * b + h + 1] for b in range(nz)]
        peak = functools.reduce(jnp.maximum, peaks)
        total = jnp.zeros((rows, 1), F32)
        summed = jnp.zeros((rows, HD), F32)
        for b in range(nz):
            f = jnp.exp2(peaks[b] - peak)
            total = total + turned[:, 8 * b + h + 2 : 8 * b + h + 3] * f
            summed = summed + z_in[b, :, pl.ds(h * HD, HD)].astype(F32) * f
        att[:, pl.ds(h * HD, HD)] = (summed / total).astype(BF16)
    swap = remote(att, att_pair, att_send, att_recv, ctx=pair)
    swap.start()
    for b in range(nz):
        pltpu.make_async_copy(
            proj_hbm.at[:, blk(2 * b + core, cw)], wo.at[b], wo_load
        ).wait()
    wait_for(wo_pair, wo_recv)
    swap.wait_recv()
    mine, theirs = att[...], att_pair[...]
    for t in range(1, nz):
        there = nearest(t, z, nz)
        c_out[there] = (dot(mine, wo[there]) + dot(theirs, wo_pair[there])).astype(BF16)
        remote(
            c_out.at[there], c_in.at[z], c_send.at[there], c_recv.at[z], ctx=2 * there + core
        ).start()
    total = dot(mine, wo[z]) + dot(theirs, wo_pair[z]) + sin[...].astype(F32)
    for t in range(1, nz):
        source = nearest(t, z, nz)
        wait_for(c_in.at[source], c_recv.at[source])
        total = total + c_in[source].astype(F32)
    out_ref[...] = total.astype(BF16)

    swap.wait_send()
    wait_for(wo_pair, wo_send)
    for i in range(ng):
        wait_for(pair_out.at[i], pair_send.at[i])
        wait_for(stat.at[i], stat_send.at[i])
    for t in range(1, nz):
        there = (z + t) % nz
        wait_for(z_out.at[there], z_send.at[there])
        wait_for(zs_out.at[there], zs_send.at[there])
        wait_for(c_out.at[there], c_send.at[there])


def expert_kernel(
    dims,
    stream_ref,
    ids_ref,
    gates_ref,
    gain_ref,
    in_hbm,
    down_hbm,
    out_ref,
    w_in,
    wd,
    wd_pair,
    blocks,
    place,
    combine,
    d_out,
    d_in,
    d_pair,
    squares,
    acc,
    act,
    act_pair,
    r_out,
    r_in,
    f_out,
    f_in,
    in_load,
    wd_load,
    wd_send,
    wd_recv,
    g_send,
    g_recv,
    d_send,
    d_recv,
    p_send,
    p_recv,
    act_send,
    act_recv,
    r_send,
    r_recv,
    f_send,
    f_recv,
):
    nz, ne, grid, rows, cw, hw = dims
    ctx, e = lax.axis_index("ctx"), lax.axis_index("exp")
    z, core = ctx // 2, ctx % 2
    pair = 2 * z + 1 - core
    slots = ne * SLOTS
    ny = grid[1]
    ex, ey = e // ny, e % ny
    peers = []
    for t in range(1, ne):
        peers.append(((ex + t // ny) % grid[0]) * ny + (ey + t % ny) % ny)

    load_in = pltpu.make_async_copy(in_hbm.at[:, 0], w_in, in_load)
    load_in.start()
    for b in range(nz):
        pltpu.make_async_copy(
            down_hbm.at[0, :, blk(2 * b + core, cw)], wd.at[b], wd_load
        ).start()

    barrier = pltpu.get_barrier_semaphore()
    pl.semaphore_signal(barrier, inc=1, device_id={"ctx": pair}, device_id_type=MESH)
    for t in range(1, nz):
        there = 2 * ((z + t) % nz) + core
        pl.semaphore_signal(barrier, inc=1, device_id={"ctx": there}, device_id_type=MESH)
    for peer in peers:
        pl.semaphore_signal(barrier, inc=1, device_id={"exp": peer}, device_id_type=MESH)
    pl.semaphore_wait(barrier, nz + ne - 1)

    for t in range(1, nz):
        there = nearest(t, z, nz)
        remote(
            stream_ref, blocks.at[z], g_send.at[there], g_recv.at[z], ctx=2 * there + core
        ).start()
    for b in range(nz):
        remote(
            down_hbm.at[0, :, blk(2 * b + 1 - core, cw)],
            wd_pair.at[b],
            wd_send,
            wd_recv,
            ctx=pair,
        ).start()
    blocks[z] = stream_ref[...]

    lane = lax.broadcasted_iota(jnp.int32, (rows, slots), 1)
    wanted = (lane // SLOTS) * nz + z
    hit = jnp.zeros((rows, slots), F32)
    weight = jnp.zeros((rows, slots), F32)
    ids, gates = ids_ref[...], gates_ref[...]
    for t in range(ids.shape[1]):
        same = ids[:, t : t + 1] == wanted
        hit = jnp.where(same, 1.0, hit)
        weight = jnp.where(same, gates[:, t : t + 1], weight)
    below = lax.broadcasted_iota(jnp.int32, (rows, rows), 1) < lax.broadcasted_iota(
        jnp.int32, (rows, rows), 0
    )
    rank = dot(below.astype(F32).astype(BF16), hit.astype(BF16))
    placed = jnp.where(rank == (lane % SLOTS).astype(F32), hit, 0.0)
    combine[...] = (placed * weight).astype(BF16)
    place[...] = placed.T.astype(BF16)
    squares[...] = jnp.zeros_like(squares)
    acc[...] = jnp.zeros_like(acc)

    def dispatch(t):
        b = nearest(t, z, nz)

        @pl.when(t > 0)
        def _():
            wait_for(blocks.at[b], g_recv.at[b])

        d_out[b] = dot(place[...], blocks[b]).astype(BF16)
        for peer in peers:
            remote(
                d_out.at[b, blk(peer, SLOTS)],
                d_in.at[b, blk(e, SLOTS)],
                d_send.at[b],
                d_recv.at[b],
                exp=peer,
            ).start()
        d_in[b, blk(e, SLOTS)] = d_out[b, blk(e, SLOTS)]

    def feed(rows_in, column):
        wide = rows_in.astype(F32)
        squared = wide * wide
        part = squares[...]
        for n in range(cw // 128):
            part = part + squared[:, n * 128 : (n + 1) * 128]
        squares[...] = part
        scaled = (wide * gain_ref[:, blk(column, cw)]).astype(BF16)
        for half in range(2):
            at = pl.ds(half * hw, hw)
            acc[:, at] = acc[:, at] + dot(scaled, w_in[half, blk(column, cw), :])

    def take(t):
        b = nearest(t, z, nz)
        got = pl.ds(0, slots - SLOTS)
        wait_for(d_in.at[b, got], d_recv.at[b])
        remote(d_in.at[b], d_pair.at[b], p_send.at[b], p_recv.at[b], ctx=pair).start()
        feed(d_in[b], 2 * b + core)

    def take_pair(t):
        b = nearest(t, z, nz)
        wait_for(d_pair.at[b], p_recv.at[b])
        feed(d_pair[b], 2 * b + 1 - core)

    lag = min(2, nz - 1)

    def lead(t, carry):
        dispatch(t)
        return carry

    lax.fori_loop(0, lag, lead, 0)
    load_in.wait()

    def turn(t, carry):
        @pl.when(t < nz)
        def _():
            dispatch(t)

        @pl.when(t < nz + lag)
        def _():
            take(t - lag)

        @pl.when(t > lag)
        def _():
            take_pair(t - lag - 1)

        return carry

    lax.fori_loop(lag, nz + lag + 1, turn, 0)

    mean = jnp.sum(squares[...], axis=1, keepdims=True) * (1.0 / (2 * nz * cw))
    inverse = lax.rsqrt(mean + 1e-6)
    gate = acc[:, pl.ds(0, hw)] * inverse
    up = acc[:, pl.ds(hw, hw)] * inverse
    act[...] = (gate / (1.0 + jnp.exp(-gate)) * up).astype(BF16)
    swap = remote(act, act_pair, act_send, act_recv, ctx=pair)
    swap.start()
    for b in range(nz):
        pltpu.make_async_copy(
            down_hbm.at[0, :, blk(2 * b + core, cw)], wd.at[b], wd_load
        ).wait()
    wait_for(wd_pair, wd_recv)
    swap.wait_recv()

    def give(t):
        b = nearest((t + 1) % nz, z, nz)
        r_out[b] = (dot(act[...], wd[b]) + dot(act_pair[...], wd_pair[b])).astype(BF16)
        for peer in peers:
            remote(
                r_out.at[b, blk(peer, SLOTS)],
                r_in.at[b, blk(e, SLOTS)],
                r_send.at[b],
                r_recv.at[b],
                exp=peer,
            ).start()
        r_in[b, blk(e, SLOTS)] = r_out[b, blk(e, SLOTS)]

    def join(t):
        b = nearest((t + 1) % nz, z, nz)
        wait_for(r_in.at[b, pl.ds(0, slots - SLOTS)], r_recv.at[b])
        f_out[b] = dot(combine[...], r_in[b]).astype(BF16)

        @pl.when(b != z)
        def _():
            remote(
                f_out.at[b], f_in.at[z], f_send.at[b], f_recv.at[z], ctx=2 * b + core
            ).start()

    def lead_back(t, carry):
        give(t)
        return carry

    lax.fori_loop(0, lag, lead_back, 0)

    def turn_back(t, carry):
        @pl.when(t < nz)
        def _():
            give(t)

        join(t - lag)
        return carry

    lax.fori_loop(lag, nz + lag, turn_back, 0)

    total = f_out[z].astype(F32)
    for t in range(1, nz):
        source = nearest(t, z, nz)
        wait_for(f_in.at[source], f_recv.at[source])
        total = total + f_in[source].astype(F32)
    out_ref[...] = (stream_ref[...].astype(F32) + total).astype(BF16)

    swap.wait_send()
    wait_for(wd_pair, wd_send)
    got = pl.ds(0, slots - SLOTS)
    for b in range(nz):
        wait_for(d_out.at[b, got], d_send.at[b])
        wait_for(r_out.at[b, got], r_send.at[b])
        wait_for(d_in.at[b], p_send.at[b])
    for t in range(1, nz):
        there = (z + t) % nz
        wait_for(blocks.at[there], g_send.at[there])
        wait_for(f_out.at[there], f_send.at[there])


def body(
    queries,
    cache_kv,
    block_kv,
    stream_in,
    out_proj,
    norm_gain,
    expert_ids,
    gate_weights,
    expert_in,
    expert_out,
):
    ctx_size, ne = lax.axis_size("ctx"), lax.axis_size("exp")
    nz = ctx_size // 2
    rows, width = queries.shape
    seqs = cache_kv.shape[1]
    masked = rows // seqs
    kvh = cache_kv.shape[3] // HD
    group = width // HD // kvh
    ng, cw, hw = kvh, width // ctx_size, expert_in.shape[3]
    slots = ne * SLOTS
    grid = (4, 4) if ne == 16 else (1, ne)
    dma, anyspace, vmem = (
        pltpu.SemaphoreType.DMA,
        pl.BlockSpec(memory_space=pl.ANY),
        pl.BlockSpec(memory_space=pltpu.VMEM),
    )
    V = pltpu.VMEM
    stream = pl.pallas_call(
        functools.partial(attention_kernel, (nz, ng, seqs, masked, group, cw)),
        out_shape=jax.ShapeDtypeStruct((rows, cw), BF16),
        in_specs=[anyspace, anyspace, vmem, anyspace, anyspace],
        out_specs=vmem,
        scratch_shapes=[
            V((rows, width), BF16),
            V(cache_kv.shape, BF16),
            V((rows, cw), BF16),
            V((nz, 2 * HD, cw), BF16),
            V((nz, 2 * HD, cw), BF16),
            V((ng, rows, 128), F32),
            V((ng, rows, 128), F32),
            V((ng, rows, 4 * HD), F32),
            V((ng, rows, 4 * HD), BF16),
            V((ng, rows, 4 * HD), BF16),
            V((nz, rows, 2 * HD), BF16),
            V((nz, rows, 2 * HD), BF16),
            V((nz, 8, rows), F32),
            V((nz, 8, rows), F32),
            V((rows, 2 * HD), BF16),
            V((rows, 2 * HD), BF16),
            V((nz, rows, cw), BF16),
            V((nz, rows, cw), BF16),
            dma((3,)),
            dma(()),
            dma(()),
            dma(()),
            dma((ng,)),
            dma((ng,)),
            dma((ng,)),
            dma((ng,)),
            dma((nz,)),
            dma((nz,)),
            dma((nz,)),
            dma((nz,)),
            dma(()),
            dma(()),
            dma((nz,)),
            dma((nz,)),
        ],
        compiler_params=pltpu.CompilerParams(
            collective_id=1, has_side_effects=True, vmem_limit_bytes=VMEM_LIMIT
        ),
    )(queries, cache_kv, block_kv, stream_in, out_proj)
    return pl.pallas_call(
        functools.partial(expert_kernel, (nz, ne, grid, rows, cw, hw)),
        out_shape=jax.ShapeDtypeStruct((rows, cw), BF16),
        in_specs=[vmem, vmem, vmem, vmem, anyspace, anyspace],
        out_specs=vmem,
        scratch_shapes=[
            V((2, width, hw), BF16),
            V((nz, hw, cw), BF16),
            V((nz, hw, cw), BF16),
            V((nz, rows, cw), BF16),
            V((slots, rows), BF16),
            V((rows, slots), BF16),
            V((nz, slots, cw), BF16),
            V((nz, slots, cw), BF16),
            V((nz, slots, cw), BF16),
            V((slots, 128), F32),
            V((slots, 2 * hw), F32),
            V((slots, hw), BF16),
            V((slots, hw), BF16),
            V((nz, slots, cw), BF16),
            V((nz, slots, cw), BF16),
            V((nz, rows, cw), BF16),
            V((nz, rows, cw), BF16),
            dma(()),
            dma(()),
            dma(()),
            dma(()),
            dma((nz,)),
            dma((nz,)),
            dma((nz,)),
            dma((nz,)),
            dma((nz,)),
            dma((nz,)),
            dma(()),
            dma(()),
            dma((nz,)),
            dma((nz,)),
            dma((nz,)),
            dma((nz,)),
        ],
        compiler_params=pltpu.CompilerParams(
            collective_id=2, has_side_effects=True, vmem_limit_bytes=VMEM_LIMIT
        ),
    )(stream, expert_ids, gate_weights, norm_gain.reshape(1, width), expert_in, expert_out)


def solution(mesh):
    placed = (
        P("exp", None),
        P(None, "exp", "ctx", None),
        P(None, "exp", "ctx", None),
        P("exp", None),
        P("ctx", None),
        P(),
        P("exp", None),
        P("exp", None),
        P(None, "exp", None, "ctx"),
        P("exp", "ctx", None),
    )
    return jax.shard_map(
        body, mesh=mesh, in_specs=placed, out_specs=P("exp", "ctx"), check_vma=False
    )
```

time: 359 us -> 110 us (0.31)
  the two profiles are of different devices: /device:TPU:1 before, /device:TPU:32 now
where the time goes in v1:
time: 110 us; the launch traced here: 109 us
  Pallas kernels  106 us (96%)
  local copies, waits for them, and re-layouts  2.93 us (3%)
    pallas_call x1, Pallas kernels, body(): pl.pallas_call(functools.partial(expert_kernel, (nz, ne, grid, rows, cw,...  61.3 us
    pallas_call x1, Pallas kernels, body(): pl.pallas_call(functools.partial(attention_kernel, (nz, ng, seqs, masked,...  45 us
    unnamed x7, local copies, waits for them, and re-layouts  2.93 us

profile of v1, /device:TPU:32, one launch (start us, length us, event | category | flops | bytes accessed | tf_op | source)
XLA Modules:
  0.0 109.3 jit_solution(3636607111660512042)
XLA Ops:
  0.0 0.0 copy-start
  0.0 0.0 copy-start.1
  0.0 45.0 %shard_map.100.stream_ref = bf16[128,256]{1,0:T(8,128)(2,1)} custom-call(bf16[128,4096]{1,0:T(8,128)(2,1)} %q_hbm.1, bf16[2,4,256,512]{3,2,1,0:T(8,128)(2,1)} %cache_hbm.1, bf16[2,4,2,512]{3,2,1,0:T(2,128)(2,1)} %block_ref.1, bf16[128,4096]{1,0:T(8,128)(2,1)} %stream_hbm.1, bf16[256,4096]{1,0:T(8,128)(2,1)} %proj_hbm.1), custom_call_target="tpu_custom_call" | custom-call | tf_op jit(solution)/shard_map/pallas_call | solution.py:560
  45.1 0.0 copy-done
  45.1 0.7 copy.11.ids_ref
  45.8 0.0 copy-done.1
  45.8 0.7 copy.12.gates_ref
  46.5 61.3 %shard_map.101 = bf16[128,256]{1,0:T(8,128)(2,1)} custom-call(bf16[128,256]{1,0:T(8,128)(2,1)} %shard_map.100.stream_ref, s32[128,8]{1,0:T(8,128)} %copy.11.ids_ref, f32[128,8]{1,0:T(8,128)} %copy.12.gates_ref, f32[1,4096]{1,0:T(1,128)} %bitcast.1, bf16[2,1,4096,256]{3,2,1,0:T(8,128)(2,1)} %in_hbm.1, bf16[1,256,4096]{2,1,0:T(8,128)(2,1)} %down_hbm.1), custom_call_target="tpu_custom_call" | custom-call | tf_op jit(solution)/shard_map/pallas_call | solution.py:605
  107.8 1.5 %copy.14 = bf16[128,256]{1,0:T(8,128)(2,1)} copy(bf16[128,256]{1,0:T(8,128)(2,1)} %shard_map.101) | data formatting | bytes 131072
Async XLA Ops:
  0.0 45.1 %copy-start = (s32[128,8]{0,1:T(8,128)S(1)}, s32[128,8]{0,1:T(8,128)}, u32[]{:S(2)}) copy-start(s32[128,8]{0,1:T(8,128)} %param.16) | copy-start | bytes 12292
  0.0 45.8 %copy-start.1 = (f32[128,8]{0,1:T(8,128)S(1)}, f32[128,8]{0,1:T(8,128)}, u32[]{:S(2)}) copy-start(f32[128,8]{0,1:T(8,128)} %param.17) | copy-start | bytes 12292

commit v2 on v0

v2 whole, which is shorter than its diff:
```python
import functools
import math

import jax
import jax.numpy as jnp
from jax import lax
from jax.experimental import pallas as pl
from jax.experimental.pallas import tpu as pltpu
from jax.sharding import PartitionSpec as P

HD = 128
SLOTS = 16
PARTS = 2
MESH = pl.DeviceIdType.MESH
F32 = jnp.float32
BF16 = jnp.bfloat16
VMEM_LIMIT = 60 * 1024 * 1024


def dot(a, b):
    return jnp.dot(a, b, preferred_element_type=F32)


def remote(src, dst, send_sem, recv_sem, **where):
    return pltpu.make_async_remote_copy(
        src_ref=src,
        dst_ref=dst,
        send_sem=send_sem,
        recv_sem=recv_sem,
        device_id=where,
        device_id_type=MESH,
    )


def wait_for(ref, sem):
    pltpu.make_async_copy(ref, ref, sem).wait()


def blk(index, size):
    return pl.ds(pl.multiple_of(index * size, size), size)


def nearest(step, here, count):
    odd = step % 2
    return (here + odd * ((step + 1) // 2) + (1 - odd) * (count - step // 2)) % count


def layer_kernel(
    dims,
    q_hbm,
    cache_hbm,
    block_ref,
    stream_hbm,
    proj_hbm,
    gain_ref,
    ids_ref,
    gates_ref,
    in_hbm,
    down_hbm,
    out_ref,
    q,
    kv,
    sin,
    wo,
    w_in,
    wd,
    stat,
    stat_pair,
    own_o,
    pair_out,
    pair_in,
    z_out,
    z_in,
    zs_out,
    zs_in,
    att,
    c_out,
    c_in,
    stream,
    blocks,
    place,
    combine,
    d_out,
    d_in,
    squares,
    acc,
    act,
    r_out,
    r_in,
    f_out,
    f_in,
    q_load,
    kv_load,
    sin_load,
    wo_load,
    wo_send,
    wo_recv,
    in_load,
    wd_load,
    wd_send,
    wd_recv,
    stat_send,
    stat_recv,
    pair_send,
    pair_recv,
    z_send,
    z_recv,
    zs_send,
    zs_recv,
    att_send,
    att_recv,
    c_send,
    c_recv,
    g_send,
    g_recv,
    d_send,
    d_recv,
    p_send,
    p_recv,
    act_send,
    act_recv,
    r_send,
    r_recv,
    f_send,
    f_recv,
):
    nz, ng, ne, grid, seqs, masked, group, cw, hw = dims
    ctx, e = lax.axis_index("ctx"), lax.axis_index("exp")
    z, core = ctx // 2, ctx % 2
    pair = 2 * z + 1 - core
    rows = seqs * masked
    span = seqs // PARTS
    pr = rows // PARTS
    steps = PARTS * ng
    slots = ne * SLOTS
    mine = blk(core, cw)
    factor = HD**-0.5 * math.log2(math.e)
    ny = grid[1]
    ex, ey = e // ny, e % ny
    peers = []
    for t in range(1, ne):
        peers.append(((ex + t // ny) % grid[0]) * ny + (ey + t % ny) % ny)

    def part_load(p):
        return (
            pltpu.make_async_copy(
                q_hbm.at[blk(p, pr)], q.at[blk(p, pr)], q_load.at[p]
            ),
            pltpu.make_async_copy(
                cache_hbm.at[:, pl.ds(p * span, span)],
                kv.at[:, pl.ds(p * span, span)],
                kv_load.at[p],
            ),
        )

    for p in range(PARTS):
        for copy in part_load(p):
            copy.start()

    barrier = pltpu.get_barrier_semaphore()
    pl.semaphore_signal(barrier, inc=1, device_id={"ctx": pair}, device_id_type=MESH)
    for t in range(1, nz):
        there = 2 * ((z + t) % nz) + core
        pl.semaphore_signal(barrier, inc=1, device_id={"ctx": there}, device_id_type=MESH)
    for peer in peers:
        pl.semaphore_signal(barrier, inc=1, device_id={"exp": peer}, device_id_type=MESH)

    load_sin = pltpu.make_async_copy(stream_hbm.at[:, blk(ctx, cw)], sin, sin_load)
    load_sin.start()
    for b in range(nz):
        pltpu.make_async_copy(
            proj_hbm.at[:, blk(2 * b + core, cw)], wo.at[b, blk(core, 2 * HD)], wo_load
        ).start()
    for half in range(2):
        pltpu.make_async_copy(
            in_hbm.at[half, 0], w_in.at[:, pl.ds(half * hw, hw)], in_load.at[half]
        ).start()
    for b in range(nz):
        pltpu.make_async_copy(
            down_hbm.at[0, :, blk(2 * b + core, cw)], wd.at[b, blk(core, hw)], wd_load
        ).start()

    pl.semaphore_wait(barrier, nz + ne - 1)

    for b in range(nz):
        remote(
            proj_hbm.at[:, blk(2 * b + 1 - core, cw)],
            wo.at[b, blk(core, 2 * HD)],
            wo_send,
            wo_recv,
            ctx=pair,
        ).start()

    lane = lax.broadcasted_iota(jnp.int32, (masked, 128), 1)

    def attend(k):
        p, i = k // ng, k % ng
        j = (z // 2 + ng // 2 + i) % ng

        @pl.when(i == 0)
        def _():
            for copy in part_load(p):
                copy.wait()

        for n in range(span):
            s = p * span + n
            here = blk(s, masked)
            local = pl.ds(n * masked, masked)
            keys = kv[0, s, :, blk(j, HD)]
            values = kv[1, s, :, blk(j, HD)]
            block_keys = block_ref[0, s, :, blk(j, HD)].astype(F32)
            block_values = block_ref[1, s, :, blk(j, HD)].astype(F32)
            heads = []
            for side in range(2):
                part = core + side - 2 * core * side
                for m in range(group // 2):
                    heads.append(j * group + (m // 2) * 4 + 2 * part + m % 2)
            qs = jnp.concatenate([q[here, blk(h, HD)] for h in heads], axis=0)
            scores = (
                lax.dot_general(
                    qs, keys, (((1,), (1,)), ((), ())), preferred_element_type=F32
                )
                * factor
            )
            qf = qs.astype(F32)
            peak = jnp.max(scores, axis=1, keepdims=True)
            extra = []
            for m in range(block_keys.shape[0]):
                one = jnp.sum(qf * block_keys[m : m + 1], axis=1, keepdims=True) * factor
                extra.append(one)
                peak = jnp.maximum(peak, one)
            weights = jnp.exp2(scores - peak)
            total = jnp.sum(weights, axis=1, keepdims=True)
            summed = dot(weights.astype(BF16), values)
            for m in range(block_keys.shape[0]):
                w = jnp.exp2(extra[m] - peak)
                total = total + w
                summed = summed + w.astype(BF16).astype(F32) * block_values[m : m + 1]
            stats = jnp.zeros((masked, 128), F32)
            for m in range(group):
                side, zz, h = m // 4, (m % 4) // 2, m % 2
                cut = slice(m * masked, (m + 1) * masked)
                at = side * 16 + zz * 8 + h
                stats = jnp.where(lane == at, peak[cut], stats)
                stats = jnp.where(lane == at + 2, total[cut], stats)
                spot = pl.ds((m % 4) * HD, HD)
                if side == 0:
                    own_o[k, local, spot] = summed[cut]
                else:
                    pair_out[k, local, spot] = summed[cut].astype(BF16)
            stat[k, local, :] = stats
        remote(
            pair_out.at[k], pair_in.at[k], pair_send.at[k], pair_recv.at[k], ctx=pair
        ).start()
        remote(
            stat.at[k], stat_pair.at[k], stat_send.at[k], stat_recv.at[k], ctx=pair
        ).start()

    lane_part = lax.broadcasted_iota(jnp.int32, (pr, 128), 1)

    def merge(k):
        p, i = k // ng, k % ng
        j = (z // 2 + ng // 2 + i) % ng
        wait_for(pair_in.at[k], pair_recv.at[k])
        wait_for(stat_pair.at[k], stat_recv.at[k])
        ours, theirs = stat[k], stat_pair[k]
        merged = jnp.zeros((pr, 128), F32)
        for zz in range(2):
            for h in range(2):
                at = zz * 8 + h
                m0, m1 = ours[:, at : at + 1], theirs[:, at + 16 : at + 17]
                l0, l1 = ours[:, at + 2 : at + 3], theirs[:, at + 18 : at + 19]
                peak = jnp.maximum(m0, m1)
                f0, f1 = jnp.exp2(m0 - peak), jnp.exp2(m1 - peak)
                merged = jnp.where(lane_part == at, peak, merged)
                merged = jnp.where(lane_part == at + 2, l0 * f0 + l1 * f1, merged)
                spot = pl.ds((zz * 2 + h) * HD, HD)
                both = own_o[k, :, spot] * f0 + pair_in[k, :, spot].astype(F32) * f1
                z_out[p, 2 * j + zz, :, pl.ds(h * HD, HD)] = both.astype(BF16)
        turned = jnp.concatenate([merged, jnp.zeros((128 - pr, 128), F32)], axis=0).T
        for zz in range(2):
            there = 2 * j + zz
            zs_out[p, there] = turned[zz * 8 : zz * 8 + 8]

            @pl.when(there == z)
            def _():
                z_in[p, there] = z_out[p, there]
                zs_in[p, there] = zs_out[p, there]

            @pl.when(there != z)
            def _():
                remote(
                    z_out.at[p, there],
                    z_in.at[p, z],
                    z_send.at[p, there],
                    z_recv.at[p, z],
                    ctx=2 * there + core,
                ).start()
                remote(
                    zs_out.at[p, there],
                    zs_in.at[p, z],
                    zs_send.at[p, there],
                    zs_recv.at[p, z],
                    ctx=2 * there + core,
                ).start()

    attend(0)

    def turn(k, carry):
        attend(k)
        merge(k - 1)
        return carry

    lax.fori_loop(1, steps, turn, 0)
    merge(steps - 1)

    def finish_heads(p):
        for t in range(1, nz):
            source = (z + t) % nz
            wait_for(z_in.at[p, source], z_recv.at[p, source])
            wait_for(zs_in.at[p, source], zs_recv.at[p, source])
        turned = jnp.concatenate([zs_in[p, b] for b in range(nz)], axis=0).T
        here = pl.ds(p * pr, pr)
        for h in range(2):
            peaks = [turned[:pr, 8 * b + h : 8 * b + h + 1] for b in range(nz)]
            peak = functools.reduce(jnp.maximum, peaks)
            total = jnp.zeros((pr, 1), F32)
            summed = jnp.zeros((pr, HD), F32)
            for b in range(nz):
                f = jnp.exp2(peaks[b] - peak)
                total = total + turned[:pr, 8 * b + h + 2 : 8 * b + h + 3] * f
                summed = summed + z_in[p, b, :, pl.ds(h * HD, HD)].astype(F32) * f
            att[here, blk(2 * core + h, HD)] = (summed / total).astype(BF16)
        return remote(
            att.at[here, mine], att.at[here, mine], att_send.at[p], att_recv.at[p], ctx=pair
        )

    def project(p):
        here = pl.ds(p * pr, pr)
        wait_for(att.at[here, mine], att_recv.at[p])
        heads = att[here, :]
        for t in range(1, nz):
            there = nearest(nz - t, z, nz)
            c_out[p, there] = dot(heads, wo[there]).astype(BF16)
            remote(
                c_out.at[p, there],
                c_in.at[p, z],
                c_send.at[p, there],
                c_recv.at[p, z],
                ctx=2 * there + core,
            ).start()

    def finish_stream(p):
        here = pl.ds(p * pr, pr)
        total = dot(att[here, :], wo[z]) + sin[here, :].astype(F32)
        for t in range(1, nz):
            source = nearest(t, z, nz)
            wait_for(c_in.at[p, source], c_recv.at[p, source])
            total = total + c_in[p, source].astype(F32)
        stream[here, :] = total.astype(BF16)
        for t in range(1, nz):
            there = nearest(t, z, nz)
            remote(
                stream.at[here],
                blocks.at[z, here],
                g_send.at[p, there],
                g_recv.at[p, z],
                ctx=2 * there + core,
            ).start()

    load_sin.wait()
    wait_for(wo.at[:, blk(core, 2 * HD)], wo_load)
    for p in range(PARTS):
        finish_heads(p).start()
        if p == 0:
            wait_for(wo.at[:, blk(core, 2 * HD)], wo_recv)
        project(p)

    for b in range(nz):
        remote(
            down_hbm.at[0, :, blk(2 * b + 1 - core, cw)],
            wd.at[b, blk(core, hw)],
            wd_send,
            wd_recv,
            ctx=pair,
        ).start()
    slot = lax.broadcasted_iota(jnp.int32, (slots, rows), 0)
    wanted = (slot // SLOTS) * nz + z
    hit = jnp.zeros((slots, rows), F32)
    weight = jnp.zeros((slots, rows), F32)
    ids, gates = ids_ref[...], gates_ref[...]
    for t in range(ids.shape[0]):
        same = ids[t : t + 1, :] == wanted
        hit = jnp.where(same, 1.0, hit)
        weight = jnp.where(same, gates[t : t + 1, :], weight)
    earlier = lax.broadcasted_iota(jnp.int32, (rows, rows), 0) < lax.broadcasted_iota(
        jnp.int32, (rows, rows), 1
    )
    rank = dot(hit.astype(BF16), earlier.astype(F32).astype(BF16))
    placed = jnp.where(rank == (slot % SLOTS).astype(F32), hit, 0.0)
    place[...] = placed.astype(BF16)
    combine[...] = (placed * weight).T.astype(BF16)
    squares[...] = jnp.zeros_like(squares)
    acc[...] = jnp.zeros_like(acc)

    for p in range(PARTS):
        finish_stream(p)
    blocks[z] = stream[...]

    def dispatch(t):
        b = nearest(t, z, nz)

        @pl.when(t > 0)
        def _():
            for p in range(PARTS):
                wait_for(blocks.at[b, pl.ds(p * pr, pr)], g_recv.at[p, b])

        d_out[b] = dot(place[...], blocks[b]).astype(BF16)
        for peer in peers:
            remote(
                d_out.at[b, blk(peer, SLOTS)],
                d_in.at[b, blk(e, SLOTS), mine],
                d_send.at[b],
                d_recv.at[b],
                exp=peer,
            ).start()
        d_in[b, blk(e, SLOTS), mine] = d_out[b, blk(e, SLOTS)]

    got = pl.ds(0, slots - SLOTS)

    def take(t):
        b = nearest(t, z, nz)
        wait_for(d_in.at[b, got, mine], d_recv.at[b])
        remote(
            d_in.at[b, :, mine], d_in.at[b, :, mine], p_send.at[b], p_recv.at[b], ctx=pair
        ).start()

    def feed(t):
        b = nearest(t, z, nz)
        wait_for(d_in.at[b, :, mine], p_recv.at[b])
        wide = d_in[b].astype(F32)
        squared = wide * wide
        part = squares[...]
        for n in range(2 * cw // 128):
            part = part + squared[:, n * 128 : (n + 1) * 128]
        squares[...] = part
        scaled = (wide * gain_ref[:, blk(b, 2 * cw)]).astype(BF16)
        acc[...] = acc[...] + dot(scaled, w_in[blk(b, 2 * cw), :])

    lag = min(2, nz - 1)

    def lead(t, carry):
        dispatch(t)
        return carry

    lax.fori_loop(0, lag, lead, 0)
    for half in range(2):
        pltpu.make_async_copy(
            in_hbm.at[half, 0], w_in.at[:, pl.ds(half * hw, hw)], in_load.at[half]
        ).wait()

    def turn_in(t, carry):
        @pl.when(t < nz)
        def _():
            dispatch(t)

        @pl.when(t < nz + lag)
        def _():
            take(t - lag)

        @pl.when(t > lag)
        def _():
            feed(t - lag - 1)

        return carry

    lax.fori_loop(lag, nz + lag + 1, turn_in, 0)

    mean = jnp.sum(squares[...], axis=1, keepdims=True) * (1.0 / (2 * nz * cw))
    inverse = lax.rsqrt(mean + 1e-6)
    gate = acc[:, pl.ds(0, hw)] * inverse
    up = acc[:, pl.ds(hw, hw)] * inverse
    act_mine = act.at[:, blk(core, hw)]
    act[:, blk(core, hw)] = (gate / (1.0 + jnp.exp(-gate)) * up).astype(BF16)
    remote(act_mine, act_mine, act_send, act_recv, ctx=pair).start()
    wait_for(wd.at[:, blk(core, hw)], wd_load)
    wait_for(wd.at[:, blk(core, hw)], wd_recv)
    wait_for(act_mine, act_recv)

    def give(t):
        b = nearest((t + 1) % nz, z, nz)
        r_out[b] = dot(act[...], wd[b]).astype(BF16)
        for peer in peers:
            remote(
                r_out.at[b, blk(peer, SLOTS)],
                r_in.at[b, blk(e, SLOTS)],
                r_send.at[b],
                r_recv.at[b],
                exp=peer,
            ).start()
        r_in[b, blk(e, SLOTS)] = r_out[b, blk(e, SLOTS)]

    def join(t):
        b = nearest((t + 1) % nz, z, nz)
        wait_for(r_in.at[b, got], r_recv.at[b])
        f_out[b] = dot(combine[...], r_in[b]).astype(BF16)

        @pl.when(b != z)
        def _():
            remote(
                f_out.at[b], f_in.at[z], f_send.at[b], f_recv.at[z], ctx=2 * b + core
            ).start()

    def lead_back(t, carry):
        give(t)
        return carry

    lax.fori_loop(0, lag, lead_back, 0)

    def turn_back(t, carry):
        @pl.when(t < nz)
        def _():
            give(t)

        join(t - lag)
        return carry

    lax.fori_loop(lag, nz + lag, turn_back, 0)

    total = f_out[z].astype(F32)
    for t in range(1, nz):
        source = nearest(t, z, nz)
        wait_for(f_in.at[source], f_recv.at[source])
        total = total + f_in[source].astype(F32)
    out_ref[...] = (stream[...].astype(F32) + total).astype(BF16)

    wait_for(wo.at[:, blk(core, 2 * HD)], wo_send)
    wait_for(wd.at[:, blk(core, hw)], wd_send)
    wait_for(act_mine, act_send)

    def drain_pair(k, carry):
        wait_for(pair_out.at[k], pair_send.at[k])
        wait_for(stat.at[k], stat_send.at[k])
        return carry

    lax.fori_loop(0, steps, drain_pair, 0)

    def drain_block(b, carry):
        wait_for(d_out.at[b, got], d_send.at[b])
        wait_for(r_out.at[b, got], r_send.at[b])
        wait_for(d_in.at[b, :, mine], p_send.at[b])
        return carry

    lax.fori_loop(0, nz, drain_block, 0)

    def drain_z(t, carry):
        there = (z + t) % nz
        wait_for(f_out.at[there], f_send.at[there])
        for p in range(PARTS):
            here = pl.ds(p * pr, pr)
            wait_for(z_out.at[p, there], z_send.at[p, there])
            wait_for(zs_out.at[p, there], zs_send.at[p, there])
            wait_for(c_out.at[p, there], c_send.at[p, there])
            wait_for(stream.at[here], g_send.at[p, there])
        return carry

    lax.fori_loop(1, nz, drain_z, 0)
    for p in range(PARTS):
        wait_for(att.at[pl.ds(p * pr, pr), mine], att_send.at[p])


def body(
    queries,
    cache_kv,
    block_kv,
    stream_in,
    out_proj,
    norm_gain,
    expert_ids,
    gate_weights,
    expert_in,
    expert_out,
):
    ctx_size, ne = lax.axis_size("ctx"), lax.axis_size("exp")
    nz = ctx_size // 2
    rows, width = queries.shape
    seqs = cache_kv.shape[1]
    masked = rows // seqs
    ng = cache_kv.shape[3] // HD
    group = width // HD // ng
    cw, hw = width // ctx_size, expert_in.shape[3]
    slots = ne * SLOTS
    grid = (4, 4) if ne == 16 else (1, ne)
    steps, pr = PARTS * ng, rows // PARTS
    dma, vm = pltpu.SemaphoreType.DMA, pltpu.VMEM
    anyspace = pl.BlockSpec(memory_space=pl.ANY)
    vmem = pl.BlockSpec(memory_space=pltpu.VMEM)
    dims = (nz, ng, ne, grid, seqs, masked, group, cw, hw)
    buffers = [
        vm((rows, width), BF16),
        vm(cache_kv.shape, BF16),
        vm((rows, cw), BF16),
        vm((nz, 4 * HD, cw), BF16),
        vm((width, 2 * hw), BF16),
        vm((nz, 2 * hw, cw), BF16),
        vm((steps, pr, 128), F32),
        vm((steps, pr, 128), F32),
        vm((steps, pr, 4 * HD), F32),
        vm((steps, pr, 4 * HD), BF16),
        vm((steps, pr, 4 * HD), BF16),
        vm((PARTS, nz, pr, 2 * HD), BF16),
        vm((PARTS, nz, pr, 2 * HD), BF16),
        vm((PARTS, nz, 8, 128), F32),
        vm((PARTS, nz, 8, 128), F32),
        vm((rows, 4 * HD), BF16),
        vm((PARTS, nz, pr, cw), BF16),
        vm((PARTS, nz, pr, cw), BF16),
        vm((rows, cw), BF16),
        vm((nz, rows, cw), BF16),
        vm((slots, rows), BF16),
        vm((rows, slots), BF16),
        vm((nz, slots, cw), BF16),
        vm((nz, slots, 2 * cw), BF16),
        vm((slots, 128), F32),
        vm((slots, 2 * hw), F32),
        vm((slots, 2 * hw), BF16),
        vm((nz, slots, cw), BF16),
        vm((nz, slots, cw), BF16),
        vm((nz, rows, cw), BF16),
        vm((nz, rows, cw), BF16),
    ]
    counts = [(PARTS,), (PARTS,)] + [()] * 4 + [(2,)] + [()] * 3
    counts += [(steps,)] * 4 + [(PARTS, nz)] * 4 + [(PARTS,)] * 2 + [(PARTS, nz)] * 4
    counts += [(nz,)] * 4 + [()] * 2 + [(nz,)] * 4
    return pl.pallas_call(
        functools.partial(layer_kernel, dims),
        out_shape=jax.ShapeDtypeStruct((rows, cw), BF16),
        in_specs=[anyspace, anyspace, vmem, anyspace, anyspace, vmem, vmem, vmem]
        + [anyspace, anyspace],
        out_specs=vmem,
        scratch_shapes=buffers + [dma(shape) for shape in counts],
        compiler_params=pltpu.CompilerParams(
            collective_id=1, has_side_effects=True, vmem_limit_bytes=VMEM_LIMIT
        ),
    )(
        queries,
        cache_kv,
        block_kv,
        stream_in,
        out_proj,
        norm_gain.reshape(1, width),
        expert_ids.T,
        gate_weights.T,
        expert_in,
        expert_out,
    )


def solution(mesh):
    placed = (
        P("exp", None),
        P(None, "exp", "ctx", None),
        P(None, "exp", "ctx", None),
        P("exp", None),
        P("ctx", None),
        P(),
        P("exp", None),
        P("exp", None),
        P(None, "exp", None, "ctx"),
        P("exp", "ctx", None),
    )
    return jax.shard_map(
        body, mesh=mesh, in_specs=placed, out_specs=P("exp", "ctx"), check_vma=False
    )
```

time: 359 us -> 93.5 us (0.26)
  the two profiles are of different devices: /device:TPU:1 before, /device:TPU:8 now
where the time goes in v2:
time: 93.5 us; the launch traced here: 93.3 us
  Pallas kernels  91.8 us (98%)
  local copies, waits for them, and re-layouts  1.47 us (2%)
    pallas_call x1, Pallas kernels, body(): pl.pallas_call(functools.partial(layer_kernel, dims), out_shape=jax.Shape...  91.8 us

profile of v2, /device:TPU:8, one launch (start us, length us, event | category | flops | bytes accessed | tf_op | source)
XLA Modules:
  0.0 93.3 jit_solution(9421955989670842285)
XLA Ops:
  0.0 91.8 %shard_map.100 = bf16[128,256]{1,0:T(8,128)(2,1)} custom-call(bf16[128,4096]{1,0:T(8,128)(2,1)} %q_hbm.1, bf16[2,4,256,512]{3,2,1,0:T(8,128)(2,1)} %cache_hbm.1, bf16[2,4,2,512]{3,2,1,0:T(2,128)(2,1)} %block_ref.1, bf16[128,4096]{1,0:T(8,128)(2,1)} %stream_hbm.1, bf16[256,4096]{1,0:T(8,128)(2,1)} %proj_hbm.1, f32[1,4096]{1,0:T(1,128)} %bitcast.3, ...), custom_call_target="tpu_custom_call" | custom-call | tf_op jit(solution)/shard_map/pallas_call | solution.py:635
  91.9 1.5 %copy.12 = bf16[128,256]{1,0:T(8,128)(2,1)} copy(bf16[128,256]{1,0:T(8,128)(2,1)} %shard_map.100) | data formatting | bytes 131072

commit v3 on v2

--- a/solution.py
+++ b/solution.py
@@ -19,6 +19,10 @@
 
 def dot(a, b):
     return jnp.dot(a, b, preferred_element_type=F32)
+
+
+def dot_t(a, b):
+    return lax.dot_general(a, b, (((1,), (1,)), ((), ())), preferred_element_type=F32)
 
 
 def remote(src, dst, send_sem, recv_sem, **where):
@@ -60,15 +64,13 @@
     out_ref,
     q,
     kv,
+    kv_pair,
+    block,
     sin,
     wo,
     w_in,
     wd,
     stat,
-    stat_pair,
-    own_o,
-    pair_out,
-    pair_in,
     z_out,
     z_in,
     zs_out,
@@ -99,10 +101,10 @@
     wd_load,
     wd_send,
     wd_recv,
-    stat_send,
-    stat_recv,
-    pair_send,
-    pair_recv,
+    kv_send,
+    kv_recv,
+    block_send,
+    block_recv,
     z_send,
     z_recv,
     zs_send,
@@ -141,17 +143,21 @@
     for t in range(1, ne):
         peers.append(((ex + t // ny) % grid[0]) * ny + (ey + t % ny) % ny)
 
+    def place_of(k):
+        return k // ng, (z // 2 + ng // 2 + k % ng) % ng
+
+    def piece(ref, p, half):
+        return ref.at[half, blk(p, span)]
+
     def part_load(p):
-        return (
-            pltpu.make_async_copy(
-                q_hbm.at[blk(p, pr)], q.at[blk(p, pr)], q_load.at[p]
-            ),
-            pltpu.make_async_copy(
-                cache_hbm.at[:, pl.ds(p * span, span)],
-                kv.at[:, pl.ds(p * span, span)],
-                kv_load.at[p],
-            ),
-        )
+        copies = [pltpu.make_async_copy(q_hbm.at[blk(p, pr)], q.at[blk(p, pr)], q_load.at[p])]
+        for half in range(2):
+            copies.append(
+                pltpu.make_async_copy(
+                    piece(cache_hbm, p, half), piece(kv, p, half), kv_load.at[p, half]
+                )
+            )
+        return copies
 
     for p in range(PARTS):
         for copy in part_load(p):
@@ -165,23 +171,35 @@
     for peer in peers:
         pl.semaphore_signal(barrier, inc=1, device_id={"exp": peer}, device_id_type=MESH)
 
+    block_rows = block_ref.shape[2]
+    block[:, :, pl.ds(0, 16)] = jnp.zeros((2, seqs, 16, block.shape[3]), BF16)
+    block[:, :, pl.ds(32, 96)] = jnp.zeros((2, seqs, 96, block.shape[3]), BF16)
+    for s in range(seqs):
+        for half in range(2):
+            block[half, s, pl.ds(0, block_rows), :] = block_ref[half, s]
+
+    pl.semaphore_wait(barrier, nz + ne - 1)
+
+    block_mine = block.at[:, :, pl.ds(0, 16)]
+    remote(
+        block_mine, block.at[:, :, pl.ds(16, 16)], block_send, block_recv, ctx=pair
+    ).start()
+
+    for p in range(PARTS):
+        for half in range(2):
+            remote(
+                piece(cache_hbm, p, half),
+                piece(kv_pair, p, half),
+                kv_send.at[p, half],
+                kv_recv.at[p, half],
+                ctx=pair,
+            ).start()
     load_sin = pltpu.make_async_copy(stream_hbm.at[:, blk(ctx, cw)], sin, sin_load)
     load_sin.start()
     for b in range(nz):
         pltpu.make_async_copy(
             proj_hbm.at[:, blk(2 * b + core, cw)], wo.at[b, blk(core, 2 * HD)], wo_load
         ).start()
-    for half in range(2):
-        pltpu.make_async_copy(
-            in_hbm.at[half, 0], w_in.at[:, pl.ds(half * hw, hw)], in_load.at[half]
-        ).start()
-    for b in range(nz):
-        pltpu.make_async_copy(
-            down_hbm.at[0, :, blk(2 * b + core, cw)], wd.at[b, blk(core, hw)], wd_load
-        ).start()
-
-    pl.semaphore_wait(barrier, nz + ne - 1)
-
     for b in range(nz):
         remote(
             proj_hbm.at[:, blk(2 * b + 1 - core, cw)],
@@ -192,92 +210,56 @@
         ).start()
 
     lane = lax.broadcasted_iota(jnp.int32, (masked, 128), 1)
-
-    def attend(k):
-        p, i = k // ng, k % ng
-        j = (z // 2 + ng // 2 + i) % ng
-
-        @pl.when(i == 0)
+    block_lane = lax.broadcasted_iota(jnp.int32, (group // 2 * masked, 128), 1)
+    block_live = (block_lane < 32) & (block_lane % 16 < block_rows)
+    ones_keys = jnp.ones((kv.shape[2], HD), BF16)
+    ones_block = jnp.ones((128, HD), BF16)
+    wait_for(block_mine, block_recv)
+
+    def attend(k, carry):
+        p, j = place_of(k)
+
+        @pl.when(k % ng == 0)
         def _():
             for copy in part_load(p):
                 copy.wait()
+            for half in range(2):
+                wait_for(piece(kv_pair, p, half), kv_recv.at[p, half])
 
         for n in range(span):
             s = p * span + n
             here = blk(s, masked)
             local = pl.ds(n * masked, masked)
-            keys = kv[0, s, :, blk(j, HD)]
-            values = kv[1, s, :, blk(j, HD)]
-            block_keys = block_ref[0, s, :, blk(j, HD)].astype(F32)
-            block_values = block_ref[1, s, :, blk(j, HD)].astype(F32)
-            heads = []
-            for side in range(2):
-                part = core + side - 2 * core * side
-                for m in range(group // 2):
-                    heads.append(j * group + (m // 2) * 4 + 2 * part + m % 2)
+            column = blk(j, HD)
+            heads = [j * group + (m // 2) * 4 + 2 * core + m % 2 for m in range(4)]
             qs = jnp.concatenate([q[here, blk(h, HD)] for h in heads], axis=0)
-            scores = (
-                lax.dot_general(
-                    qs, keys, (((1,), (1,)), ((), ())), preferred_element_type=F32
-                )
-                * factor
+            scores = [
+                dot_t(qs, kv[0, s, :, column]),
+                dot_t(qs, kv_pair[0, s, :, column]),
+                jnp.where(block_live, dot_t(qs, block[0, s, :, column]), -1e30),
+            ]
+            widest = scores[2]
+            for m in range(kv.shape[2] // 128):
+                cut = slice(m * 128, (m + 1) * 128)
+                widest = jnp.maximum(widest, jnp.maximum(scores[0][:, cut], scores[1][:, cut]))
+            peak = jnp.max(widest, axis=1, keepdims=True)
+            weights = [jnp.exp2((part - peak) * factor).astype(BF16) for part in scores]
+            both = dot(weights[0], jnp.concatenate([kv[1, s, :, column], ones_keys], axis=1))
+            both += dot(
+                weights[1], jnp.concatenate([kv_pair[1, s, :, column], ones_keys], axis=1)
             )
-            qf = qs.astype(F32)
-            peak = jnp.max(scores, axis=1, keepdims=True)
-            extra = []
-            for m in range(block_keys.shape[0]):
-                one = jnp.sum(qf * block_keys[m : m + 1], axis=1, keepdims=True) * factor
-                extra.append(one)
-                peak = jnp.maximum(peak, one)
-            weights = jnp.exp2(scores - peak)
-            total = jnp.sum(weights, axis=1, keepdims=True)
-            summed = dot(weights.astype(BF16), values)
-            for m in range(block_keys.shape[0]):
-                w = jnp.exp2(extra[m] - peak)
-                total = total + w
-                summed = summed + w.astype(BF16).astype(F32) * block_values[m : m + 1]
+            both += dot(weights[2], jnp.concatenate([block[1, s, :, column], ones_block], axis=1))
+            summed, total = both[:, :HD].astype(BF16), both[:, HD:]
+            peak = peak * factor
             stats = jnp.zeros((masked, 128), F32)
-            for m in range(group):
-                side, zz, h = m // 4, (m % 4) // 2, m % 2
+            for m in range(4):
+                zz, h = m // 2, m % 2
                 cut = slice(m * masked, (m + 1) * masked)
-                at = side * 16 + zz * 8 + h
-                stats = jnp.where(lane == at, peak[cut], stats)
-                stats = jnp.where(lane == at + 2, total[cut], stats)
-                spot = pl.ds((m % 4) * HD, HD)
-                if side == 0:
-                    own_o[k, local, spot] = summed[cut]
-                else:
-                    pair_out[k, local, spot] = summed[cut].astype(BF16)
-            stat[k, local, :] = stats
-        remote(
-            pair_out.at[k], pair_in.at[k], pair_send.at[k], pair_recv.at[k], ctx=pair
-        ).start()
-        remote(
-            stat.at[k], stat_pair.at[k], stat_send.at[k], stat_recv.at[k], ctx=pair
-        ).start()
-
-    lane_part = lax.broadcasted_iota(jnp.int32, (pr, 128), 1)
-
-    def merge(k):
-        p, i = k // ng, k % ng
-        j = (z // 2 + ng // 2 + i) % ng
-        wait_for(pair_in.at[k], pair_recv.at[k])
-        wait_for(stat_pair.at[k], stat_recv.at[k])
-        ours, theirs = stat[k], stat_pair[k]
-        merged = jnp.zeros((pr, 128), F32)
-        for zz in range(2):
-            for h in range(2):
-                at = zz * 8 + h
-                m0, m1 = ours[:, at : at + 1], theirs[:, at + 16 : at + 17]
-                l0, l1 = ours[:, at + 2 : at + 3], theirs[:, at + 18 : at + 19]
-                peak = jnp.maximum(m0, m1)
-                f0, f1 = jnp.exp2(m0 - peak), jnp.exp2(m1 - peak)
-                merged = jnp.where(lane_part == at, peak, merged)
-                merged = jnp.where(lane_part == at + 2, l0 * f0 + l1 * f1, merged)
-                spot = pl.ds((zz * 2 + h) * HD, HD)
-                both = own_o[k, :, spot] * f0 + pair_in[k, :, spot].astype(F32) * f1
-                z_out[p, 2 * j + zz, :, pl.ds(h * HD, HD)] = both.astype(BF16)
-        turned = jnp.concatenate([merged, jnp.zeros((128 - pr, 128), F32)], axis=0).T
+                stats = jnp.where(lane == zz * 8 + h, peak[cut], stats)
+                stats = jnp.where(lane == zz * 8 + h + 2, total[cut], stats)
+                z_out[p, 2 * j + zz, local, pl.ds(h * HD, HD)] = summed[cut]
+            stat[local, :] = stats
+        turned = stat[...].T
         for zz in range(2):
             there = 2 * j + zz
             zs_out[p, there] = turned[zz * 8 : zz * 8 + 8]
@@ -304,33 +286,41 @@
                     ctx=2 * there + core,
                 ).start()
 
-    attend(0)
-
-    def turn(k, carry):
-        attend(k)
-        merge(k - 1)
         return carry
 
-    lax.fori_loop(1, steps, turn, 0)
-    merge(steps - 1)
+    stat[...] = jnp.zeros_like(stat)
+    lax.fori_loop(0, steps, attend, 0)
+    for half in range(2):
+        pltpu.make_async_copy(
+            in_hbm.at[half, 0], w_in.at[:, pl.ds(half * hw, hw)], in_load.at[half]
+        ).start()
+    for b in range(nz):
+        pltpu.make_async_copy(
+            down_hbm.at[0, :, blk(2 * b + core, cw)], wd.at[b, blk(core, hw)], wd_load
+        ).start()
+
 
     def finish_heads(p):
         for t in range(1, nz):
             source = (z + t) % nz
             wait_for(z_in.at[p, source], z_recv.at[p, source])
             wait_for(zs_in.at[p, source], zs_recv.at[p, source])
+        here = pl.ds(p * pr, pr)
+        peaks = [zs_in[p, b, pl.ds(0, 2), :] for b in range(nz)]
+        peak = functools.reduce(jnp.maximum, peaks)
+        factors = [jnp.exp2(one - peak) for one in peaks]
+        total = jnp.zeros((2, 128), F32)
+        for b in range(nz):
+            total = total + zs_in[p, b, pl.ds(2, 2), :] * factors[b]
+        for b in range(nz):
+            zs_in[p, b, pl.ds(4, 2), :] = factors[b] / total
         turned = jnp.concatenate([zs_in[p, b] for b in range(nz)], axis=0).T
-        here = pl.ds(p * pr, pr)
         for h in range(2):
-            peaks = [turned[:pr, 8 * b + h : 8 * b + h + 1] for b in range(nz)]
-            peak = functools.reduce(jnp.maximum, peaks)
-            total = jnp.zeros((pr, 1), F32)
             summed = jnp.zeros((pr, HD), F32)
             for b in range(nz):
-                f = jnp.exp2(peaks[b] - peak)
-                total = total + turned[:pr, 8 * b + h + 2 : 8 * b + h + 3] * f
+                f = turned[:pr, 8 * b + h + 4 : 8 * b + h + 5]
                 summed = summed + z_in[p, b, :, pl.ds(h * HD, HD)].astype(F32) * f
-            att[here, blk(2 * core + h, HD)] = (summed / total).astype(BF16)
+            att[here, blk(2 * core + h, HD)] = summed.astype(BF16)
         return remote(
             att.at[here, mine], att.at[here, mine], att_send.at[p], att_recv.at[p], ctx=pair
         )
@@ -447,7 +437,7 @@
         scaled = (wide * gain_ref[:, blk(b, 2 * cw)]).astype(BF16)
         acc[...] = acc[...] + dot(scaled, w_in[blk(b, 2 * cw), :])
 
-    lag = min(2, nz - 1)
+    lag = nz // 2
 
     def lead(t, carry):
         dispatch(t)
@@ -488,7 +478,7 @@
     wait_for(act_mine, act_recv)
 
     def give(t):
-        b = nearest((t + 1) % nz, z, nz)
+        b = nearest(nz - 1 - t, z, nz)
         r_out[b] = dot(act[...], wd[b]).astype(BF16)
         for peer in peers:
             remote(
@@ -501,7 +491,7 @@
         r_in[b, blk(e, SLOTS)] = r_out[b, blk(e, SLOTS)]
 
     def join(t):
-        b = nearest((t + 1) % nz, z, nz)
+        b = nearest(nz - 1 - t, z, nz)
         wait_for(r_in.at[b, got], r_recv.at[b])
         f_out[b] = dot(combine[...], r_in[b]).astype(BF16)
 
@@ -538,12 +528,10 @@
     wait_for(wd.at[:, blk(core, hw)], wd_send)
     wait_for(act_mine, act_send)
 
-    def drain_pair(k, carry):
-        wait_for(pair_out.at[k], pair_send.at[k])
-        wait_for(stat.at[k], stat_send.at[k])
-        return carry
-
-    lax.fori_loop(0, steps, drain_pair, 0)
+    for p in range(PARTS):
+        for half in range(2):
+            wait_for(piece(kv, p, half), kv_send.at[p, half])
+    wait_for(block_mine, block_send)
 
     def drain_block(b, carry):
         wait_for(d_out.at[b, got], d_send.at[b])
@@ -599,15 +587,13 @@
     buffers = [
         vm((rows, width), BF16),
         vm(cache_kv.shape, BF16),
+        vm(cache_kv.shape, BF16),
+        vm((2, seqs, 128, cache_kv.shape[3]), BF16),
         vm((rows, cw), BF16),
         vm((nz, 4 * HD, cw), BF16),
         vm((width, 2 * hw), BF16),
         vm((nz, 2 * hw, cw), BF16),
-        vm((steps, pr, 128), F32),
-        vm((steps, pr, 128), F32),
-        vm((steps, pr, 4 * HD), F32),
-        vm((steps, pr, 4 * HD), BF16),
-        vm((steps, pr, 4 * HD), BF16),
+        vm((128, 128), F32),
         vm((PARTS, nz, pr, 2 * HD), BF16),
         vm((PARTS, nz, pr, 2 * HD), BF16),
         vm((PARTS, nz, 8, 128), F32),
@@ -629,8 +615,8 @@
         vm((nz, rows, cw), BF16),
         vm((nz, rows, cw), BF16),
     ]
-    counts = [(PARTS,), (PARTS,)] + [()] * 4 + [(2,)] + [()] * 3
-    counts += [(steps,)] * 4 + [(PARTS, nz)] * 4 + [(PARTS,)] * 2 + [(PARTS, nz)] * 4
+    counts = [(PARTS,), (PARTS, 2)] + [()] * 4 + [(2,)] + [()] * 3
+    counts += [(PARTS, 2)] * 2 + [()] * 2 + [(PARTS, nz)] * 4 + [(PARTS,)] * 2 + [(PARTS, nz)] * 4
     counts += [(nz,)] * 4 + [()] * 2 + [(nz,)] * 4
     return pl.pallas_call(
         functools.partial(layer_kernel, dims),

time: 93.5 us -> 87.1 us (0.932)
  the two profiles are of different devices: /device:TPU:8 before, /device:TPU:1 now
where the time goes in v3:
time: 87.1 us; the launch traced here: 86.9 us
  Pallas kernels  85.4 us (98%)
  local copies, waits for them, and re-layouts  1.47 us (2%)
    pallas_call x1, Pallas kernels, body(): pl.pallas_call(functools.partial(layer_kernel, dims), out_shape=jax.Shape...  85.4 us

profile of v3, /device:TPU:1, one launch (start us, length us, event | category | flops | bytes accessed | tf_op | source)
XLA Modules:
  0.0 86.9 jit_solution(2652106352197117765)
XLA Ops:
  0.0 85.4 %shard_map.100 = bf16[128,256]{1,0:T(8,128)(2,1)} custom-call(bf16[128,4096]{1,0:T(8,128)(2,1)} %q_hbm.1, bf16[2,4,256,512]{3,2,1,0:T(8,128)(2,1)} %cache_hbm.1, bf16[2,4,2,512]{3,2,1,0:T(2,128)(2,1)} %block_ref.1, bf16[128,4096]{1,0:T(8,128)(2,1)} %stream_hbm.1, bf16[256,4096]{1,0:T(8,128)(2,1)} %proj_hbm.1, f32[1,4096]{1,0:T(1,128)} %bitcast.3, ...), custom_call_target="tpu_custom_call" | custom-call | tf_op jit(solution)/shard_map/pallas_call | solution.py:621
  85.4 1.5 %copy.12 = bf16[128,256]{1,0:T(8,128)(2,1)} copy(bf16[128,256]{1,0:T(8,128)(2,1)} %shard_map.100) | data formatting | bytes 131072

commit v4 on v3

--- a/solution.py
+++ b/solution.py
@@ -115,6 +115,7 @@
     c_recv,
     g_send,
     g_recv,
+    h_send,
     d_send,
     d_recv,
     p_send,
@@ -140,7 +141,8 @@
     ny = grid[1]
     ex, ey = e // ny, e % ny
     peers = []
-    for t in range(1, ne):
+    steps_away = [min(t // ny, grid[0] - t // ny) + min(t % ny, ny - t % ny) for t in range(ne)]
+    for t in sorted(range(1, ne), key=lambda t: -steps_away[t]):
         peers.append(((ex + t // ny) % grid[0]) * ny + (ey + t % ny) % ny)
 
     def place_of(k):
@@ -348,7 +350,7 @@
             wait_for(c_in.at[p, source], c_recv.at[p, source])
             total = total + c_in[p, source].astype(F32)
         stream[here, :] = total.astype(BF16)
-        for t in range(1, nz):
+        for t in range(1, min(nz, 5)):
             there = nearest(t, z, nz)
             remote(
                 stream.at[here],
@@ -357,6 +359,28 @@
                 g_recv.at[p, z],
                 ctx=2 * there + core,
             ).start()
+
+    def hand_on(b, first, second):
+        for p in range(PARTS):
+            here = pl.ds(p * pr, pr)
+            there = (z + first) % nz
+            remote(
+                blocks.at[b, here],
+                blocks.at[b, here],
+                h_send.at[p, there],
+                g_recv.at[p, b],
+                ctx=2 * there + core,
+            ).start()
+        here = pl.ds((first == 1) * pr, pr)
+        there = (z + second) % nz
+        part = int(first == 1)
+        remote(
+            blocks.at[b, here],
+            blocks.at[b, here],
+            h_send.at[part, there],
+            g_recv.at[part, b],
+            ctx=2 * there + core,
+        ).start()
 
     load_sin.wait()
     wait_for(wo.at[:, blk(core, 2 * HD)], wo_load)
@@ -405,6 +429,16 @@
             for p in range(PARTS):
                 wait_for(blocks.at[b, pl.ds(p * pr, pr)], g_recv.at[p, b])
 
+        if nz == 8:
+
+            @pl.when(t == 3)
+            def _():
+                hand_on(b, nz - 1, nz - 2)
+
+            @pl.when(t == 4)
+            def _():
+                hand_on(b, 1, 2)
+
         d_out[b] = dot(place[...], blocks[b]).astype(BF16)
         for peer in peers:
             remote(
@@ -549,10 +583,17 @@
             wait_for(z_out.at[p, there], z_send.at[p, there])
             wait_for(zs_out.at[p, there], zs_send.at[p, there])
             wait_for(c_out.at[p, there], c_send.at[p, there])
+        return carry
+
+    lax.fori_loop(1, nz, drain_z, 0)
+    for p in range(PARTS):
+        here = pl.ds(p * pr, pr)
+        for t in range(1, min(nz, 5)):
+            there = nearest(t, z, nz)
             wait_for(stream.at[here], g_send.at[p, there])
-        return carry
-
-    lax.fori_loop(1, nz, drain_z, 0)
+        if nz == 8:
+            for t in (1, nz - 1, 2 if p == 1 else nz - 2):
+                wait_for(stream.at[here], h_send.at[p, (z + t) % nz])
     for p in range(PARTS):
         wait_for(att.at[pl.ds(p * pr, pr), mine], att_send.at[p])
 
@@ -616,7 +657,7 @@
         vm((nz, rows, cw), BF16),
     ]
     counts = [(PARTS,), (PARTS, 2)] + [()] * 4 + [(2,)] + [()] * 3
-    counts += [(PARTS, 2)] * 2 + [()] * 2 + [(PARTS, nz)] * 4 + [(PARTS,)] * 2 + [(PARTS, nz)] * 4
+    counts += [(PARTS, 2)] * 2 + [()] * 2 + [(PARTS, nz)] * 4 + [(PARTS,)] * 2 + [(PARTS, nz)] * 5
     counts += [(nz,)] * 4 + [()] * 2 + [(nz,)] * 4
     return pl.pallas_call(
         functools.partial(layer_kernel, dims),

time: 87.1 us -> 83.5 us (0.959)
  Pallas kernels: 85.4 us -> 81.9 us
    pallas_call x1, Pallas kernels: 85.4 us -> 81.9 us  [body(): pl.pallas_call(functools.partial(layer_kernel, dims), out_shape=jax.Shape...]
where the time goes in v4:
time: 83.5 us; the launch traced here: 83.3 us
  Pallas kernels  81.9 us (98%)
  local copies, waits for them, and re-layouts  1.47 us (2%)
    pallas_call x1, Pallas kernels, body(): pl.pallas_call(functools.partial(layer_kernel, dims), out_shape=jax.Shape...  81.9 us

profile of v4, /device:TPU:1, one launch (start us, length us, event | category | flops | bytes accessed | tf_op | source)
XLA Modules:
  0.0 83.3 jit_solution(17378964881476622532)
XLA Ops:
  0.0 81.9 %shard_map.100 = bf16[128,256]{1,0:T(8,128)(2,1)} custom-call(bf16[128,4096]{1,0:T(8,128)(2,1)} %q_hbm.1, bf16[2,4,256,512]{3,2,1,0:T(8,128)(2,1)} %cache_hbm.1, bf16[2,4,2,512]{3,2,1,0:T(2,128)(2,1)} %block_ref.1, bf16[128,4096]{1,0:T(8,128)(2,1)} %stream_hbm.1, bf16[256,4096]{1,0:T(8,128)(2,1)} %proj_hbm.1, f32[1,4096]{1,0:T(1,128)} %bitcast.3, ...), custom_call_target="tpu_custom_call" | custom-call | tf_op jit(solution)/shard_map/pallas_call | solution.py:662
  81.9 1.5 %copy.12 = bf16[128,256]{1,0:T(8,128)(2,1)} copy(bf16[128,256]{1,0:T(8,128)(2,1)} %shard_map.100) | data formatting | bytes 131072

commit v5 on v4

--- a/solution.py
+++ b/solution.py
@@ -53,18 +53,22 @@
     dims,
     q_hbm,
     cache_hbm,
-    block_ref,
+    block_hbm,
     stream_hbm,
     proj_hbm,
-    gain_ref,
-    ids_ref,
-    gates_ref,
+    gain_hbm,
+    ids_hbm,
+    gates_hbm,
     in_hbm,
     down_hbm,
     out_ref,
     q,
     kv,
     kv_pair,
+    block_ref,
+    gain_ref,
+    ids_ref,
+    gates_ref,
     block,
     sin,
     wo,
@@ -91,6 +95,7 @@
     r_in,
     f_out,
     f_in,
+    small_load,
     q_load,
     kv_load,
     sin_load,
@@ -161,31 +166,34 @@
             )
         return copies
 
-    for p in range(PARTS):
-        for copy in part_load(p):
-            copy.start()
-
     barrier = pltpu.get_barrier_semaphore()
     pl.semaphore_signal(barrier, inc=1, device_id={"ctx": pair}, device_id_type=MESH)
+    for copy in part_load(0):
+        copy.start()
     for t in range(1, nz):
         there = 2 * ((z + t) % nz) + core
         pl.semaphore_signal(barrier, inc=1, device_id={"ctx": there}, device_id_type=MESH)
     for peer in peers:
         pl.semaphore_signal(barrier, inc=1, device_id={"exp": peer}, device_id_type=MESH)
 
-    block_rows = block_ref.shape[2]
-    block[:, :, pl.ds(0, 16)] = jnp.zeros((2, seqs, 16, block.shape[3]), BF16)
-    block[:, :, pl.ds(32, 96)] = jnp.zeros((2, seqs, 96, block.shape[3]), BF16)
-    for s in range(seqs):
-        for half in range(2):
-            block[half, s, pl.ds(0, block_rows), :] = block_ref[half, s]
+    for p in range(1, PARTS):
+        for copy in part_load(p):
+            copy.start()
+    small = [
+        pltpu.make_async_copy(source, here, small_load.at[n])
+        for n, (source, here) in enumerate(
+            [
+                (block_hbm, block_ref),
+                (gain_hbm, gain_ref),
+                (ids_hbm, ids_ref),
+                (gates_hbm, gates_ref),
+            ]
+        )
+    ]
+    for copy in small:
+        copy.start()
 
     pl.semaphore_wait(barrier, nz + ne - 1)
-
-    block_mine = block.at[:, :, pl.ds(0, 16)]
-    remote(
-        block_mine, block.at[:, :, pl.ds(16, 16)], block_send, block_recv, ctx=pair
-    ).start()
 
     for p in range(PARTS):
         for half in range(2):
@@ -196,6 +204,19 @@
                 kv_recv.at[p, half],
                 ctx=pair,
             ).start()
+    block_rows = block_ref.shape[2]
+    small[0].wait()
+    block[:, :, pl.ds(0, 16)] = jnp.zeros((2, seqs, 16, block.shape[3]), BF16)
+    block[:, :, pl.ds(32, 96)] = jnp.zeros((2, seqs, 96, block.shape[3]), BF16)
+    for s in range(seqs):
+        for half in range(2):
+            block[half, s, pl.ds(0, block_rows), :] = block_ref[half, s]
+
+    block_mine = block.at[:, :, pl.ds(0, 16)]
+    remote(
+        block_mine, block.at[:, :, pl.ds(16, 16)], block_send, block_recv, ctx=pair
+    ).start()
+
     load_sin = pltpu.make_async_copy(stream_hbm.at[:, blk(ctx, cw)], sin, sin_load)
     load_sin.start()
     for b in range(nz):
@@ -218,41 +239,63 @@
     ones_block = jnp.ones((128, HD), BF16)
     wait_for(block_mine, block_recv)
 
-    def attend(k, carry):
+    def await_keys(p):
+        for copy in part_load(p)[:2]:
+            copy.wait()
+        wait_for(piece(kv_pair, p, 0), kv_recv.at[p, 0])
+
+    def await_values(p):
+        part_load(p)[2].wait()
+        wait_for(piece(kv_pair, p, 1), kv_recv.at[p, 1])
+
+    def attend(k, first):
         p, j = place_of(k)
-
-        @pl.when(k % ng == 0)
-        def _():
-            for copy in part_load(p):
-                copy.wait()
-            for half in range(2):
-                wait_for(piece(kv_pair, p, half), kv_recv.at[p, half])
-
-        for n in range(span):
-            s = p * span + n
-            here = blk(s, masked)
-            local = pl.ds(n * masked, masked)
-            column = blk(j, HD)
-            heads = [j * group + (m // 2) * 4 + 2 * core + m % 2 for m in range(4)]
-            qs = jnp.concatenate([q[here, blk(h, HD)] for h in heads], axis=0)
-            scores = [
-                dot_t(qs, kv[0, s, :, column]),
-                dot_t(qs, kv_pair[0, s, :, column]),
-                jnp.where(block_live, dot_t(qs, block[0, s, :, column]), -1e30),
-            ]
-            widest = scores[2]
+        if first:
+            await_keys(0)
+        else:
+
+            @pl.when(k % ng == 0)
+            def _():
+                await_keys(p)
+                await_values(p)
+
+        column = blk(j, HD)
+        heads = [j * group + (m // 2) * 4 + 2 * core + m % 2 for m in range(4)]
+        which = [p * span + n for n in range(span)]
+        scores = []
+        for s in which:
+            qs = jnp.concatenate([q[blk(s, masked), blk(h, HD)] for h in heads], axis=0)
+            scores.append(
+                [
+                    dot_t(qs, kv[0, s, :, column]),
+                    dot_t(qs, kv_pair[0, s, :, column]),
+                    jnp.where(block_live, dot_t(qs, block[0, s, :, column]), -1e30),
+                ]
+            )
+        peaks = []
+        for own, other, extra in scores:
+            widest = extra
             for m in range(kv.shape[2] // 128):
                 cut = slice(m * 128, (m + 1) * 128)
-                widest = jnp.maximum(widest, jnp.maximum(scores[0][:, cut], scores[1][:, cut]))
-            peak = jnp.max(widest, axis=1, keepdims=True)
-            weights = [jnp.exp2((part - peak) * factor).astype(BF16) for part in scores]
-            both = dot(weights[0], jnp.concatenate([kv[1, s, :, column], ones_keys], axis=1))
+                widest = jnp.maximum(widest, jnp.maximum(own[:, cut], other[:, cut]))
+            peaks.append(jnp.max(widest, axis=1, keepdims=True))
+        weights = [
+            [jnp.exp2((part - peak) * factor).astype(BF16) for part in parts]
+            for parts, peak in zip(scores, peaks)
+        ]
+        if first:
+            await_values(0)
+        for n, s in enumerate(which):
+            local = pl.ds(n * masked, masked)
+            both = dot(weights[n][0], jnp.concatenate([kv[1, s, :, column], ones_keys], axis=1))
             both += dot(
-                weights[1], jnp.concatenate([kv_pair[1, s, :, column], ones_keys], axis=1)
+                weights[n][1], jnp.concatenate([kv_pair[1, s, :, column], ones_keys], axis=1)
             )
-            both += dot(weights[2], jnp.concatenate([block[1, s, :, column], ones_block], axis=1))
+            both += dot(
+                weights[n][2], jnp.concatenate([block[1, s, :, column], ones_block], axis=1)
+            )
             summed, total = both[:, :HD].astype(BF16), both[:, HD:]
-            peak = peak * factor
+            peak = peaks[n] * factor
             stats = jnp.zeros((masked, 128), F32)
             for m in range(4):
                 zz, h = m // 2, m % 2
@@ -288,10 +331,14 @@
                     ctx=2 * there + core,
                 ).start()
 
+    stat[...] = jnp.zeros_like(stat)
+    attend(0, True)
+
+    def turn(k, carry):
+        attend(k, False)
         return carry
 
-    stat[...] = jnp.zeros_like(stat)
-    lax.fori_loop(0, steps, attend, 0)
+    lax.fori_loop(1, steps, turn, 0)
     for half in range(2):
         pltpu.make_async_copy(
             in_hbm.at[half, 0], w_in.at[:, pl.ds(half * hw, hw)], in_load.at[half]
@@ -402,6 +449,8 @@
     wanted = (slot // SLOTS) * nz + z
     hit = jnp.zeros((slots, rows), F32)
     weight = jnp.zeros((slots, rows), F32)
+    for copy in small[1:]:
+        copy.wait()
     ids, gates = ids_ref[...], gates_ref[...]
     for t in range(ids.shape[0]):
         same = ids[t : t + 1, :] == wanted
@@ -551,13 +600,6 @@
 
     lax.fori_loop(lag, nz + lag, turn_back, 0)
 
-    total = f_out[z].astype(F32)
-    for t in range(1, nz):
-        source = nearest(t, z, nz)
-        wait_for(f_in.at[source], f_recv.at[source])
-        total = total + f_in[source].astype(F32)
-    out_ref[...] = (stream[...].astype(F32) + total).astype(BF16)
-
     wait_for(wo.at[:, blk(core, 2 * HD)], wo_send)
     wait_for(wd.at[:, blk(core, hw)], wd_send)
     wait_for(act_mine, act_send)
@@ -577,7 +619,6 @@
 
     def drain_z(t, carry):
         there = (z + t) % nz
-        wait_for(f_out.at[there], f_send.at[there])
         for p in range(PARTS):
             here = pl.ds(p * pr, pr)
             wait_for(z_out.at[p, there], z_send.at[p, there])
@@ -596,6 +637,17 @@
                 wait_for(stream.at[here], h_send.at[p, (z + t) % nz])
     for p in range(PARTS):
         wait_for(att.at[pl.ds(p * pr, pr), mine], att_send.at[p])
+
+    total = f_out[z].astype(F32)
+    for t in range(1, nz):
+        source = nearest(t, z, nz)
+        wait_for(f_in.at[source], f_recv.at[source])
+        total = total + f_in[source].astype(F32)
+    out_ref[...] = (stream[...].astype(F32) + total).astype(BF16)
+
+    for t in range(1, nz):
+        there = nearest(t, z, nz)
+        wait_for(f_out.at[there], f_send.at[there])
 
 
 def body(
@@ -629,6 +681,10 @@
         vm((rows, width), BF16),
         vm(cache_kv.shape, BF16),
         vm(cache_kv.shape, BF16),
+        vm(block_kv.shape, BF16),
+        vm((1, width), F32),
+        vm(expert_ids.shape[::-1], jnp.int32),
+        vm(gate_weights.shape[::-1], F32),
         vm((2, seqs, 128, cache_kv.shape[3]), BF16),
         vm((rows, cw), BF16),
         vm((nz, 4 * HD, cw), BF16),
@@ -656,14 +712,13 @@
         vm((nz, rows, cw), BF16),
         vm((nz, rows, cw), BF16),
     ]
-    counts = [(PARTS,), (PARTS, 2)] + [()] * 4 + [(2,)] + [()] * 3
+    counts = [(4,), (PARTS,), (PARTS, 2)] + [()] * 4 + [(2,)] + [()] * 3
     counts += [(PARTS, 2)] * 2 + [()] * 2 + [(PARTS, nz)] * 4 + [(PARTS,)] * 2 + [(PARTS, nz)] * 5
     counts += [(nz,)] * 4 + [()] * 2 + [(nz,)] * 4
     return pl.pallas_call(
         functools.partial(layer_kernel, dims),
         out_shape=jax.ShapeDtypeStruct((rows, cw), BF16),
-        in_specs=[anyspace, anyspace, vmem, anyspace, anyspace, vmem, vmem, vmem]
-        + [anyspace, anyspace],
+        in_specs=[anyspace] * 10,
         out_specs=vmem,
         scratch_shapes=buffers + [dma(shape) for shape in counts],
         compiler_params=pltpu.CompilerParams(

time: 83.5 us -> 81.5 us (0.976)
  Pallas kernels: 81.9 us -> 79.9 us
    pallas_call x1, Pallas kernels: 81.9 us -> 79.9 us  [body(): pl.pallas_call(functools.partial(layer_kernel, dims), out_shape=jax.Shape...]
where the time goes in v5:
time: 81.5 us; the launch traced here: 81.4 us
  Pallas kernels  79.9 us (98%)
  local copies, waits for them, and re-layouts  1.47 us (2%)
    pallas_call x1, Pallas kernels, body(): pl.pallas_call(functools.partial(layer_kernel, dims), out_shape=jax.Shape...  79.9 us

profile of v5, /device:TPU:1, one launch (start us, length us, event | category | flops | bytes accessed | tf_op | source)
XLA Modules:
  0.0 81.4 jit_solution(15050968831345827388)
XLA Ops:
  0.0 79.9 %shard_map.100 = bf16[128,256]{1,0:T(8,128)(2,1)} custom-call(bf16[128,4096]{1,0:T(8,128)(2,1)} %q_hbm.1, bf16[2,4,256,512]{3,2,1,0:T(8,128)(2,1)} %cache_hbm.1, bf16[2,4,2,512]{3,2,1,0:T(2,128)(2,1)} %block_hbm.1, bf16[128,4096]{1,0:T(8,128)(2,1)} %stream_hbm.1, bf16[256,4096]{1,0:T(8,128)(2,1)} %proj_hbm.1, f32[1,4096]{1,0:T(1,128)} %bitcast.3, ...), custom_call_target="tpu_custom_call" | custom-call | tf_op jit(solution)/shard_map/pallas_call | solution.py:718
  79.9 1.5 %copy.12 = bf16[128,256]{1,0:T(8,128)(2,1)} copy(bf16[128,256]{1,0:T(8,128)(2,1)} %shard_map.100) | data formatting | bytes 131072

commit v6 on v5

--- a/solution.py
+++ b/solution.py
@@ -237,11 +237,12 @@
     block_live = (block_lane < 32) & (block_lane % 16 < block_rows)
     ones_keys = jnp.ones((kv.shape[2], HD), BF16)
     ones_block = jnp.ones((128, HD), BF16)
-    wait_for(block_mine, block_recv)
 
     def await_keys(p):
         for copy in part_load(p)[:2]:
             copy.wait()
+
+    def await_pair_keys(p):
         wait_for(piece(kv_pair, p, 0), kv_recv.at[p, 0])
 
     def await_values(p):
@@ -257,21 +258,23 @@
             @pl.when(k % ng == 0)
             def _():
                 await_keys(p)
+                await_pair_keys(p)
                 await_values(p)
 
         column = blk(j, HD)
         heads = [j * group + (m // 2) * 4 + 2 * core + m % 2 for m in range(4)]
         which = [p * span + n for n in range(span)]
+        asked = [
+            jnp.concatenate([q[blk(s, masked), blk(h, HD)] for h in heads], axis=0) for s in which
+        ]
+        own_scores = [dot_t(qs, kv[0, s, :, column]) for qs, s in zip(asked, which)]
+        if first:
+            wait_for(block_mine, block_recv)
+            await_pair_keys(0)
         scores = []
-        for s in which:
-            qs = jnp.concatenate([q[blk(s, masked), blk(h, HD)] for h in heads], axis=0)
-            scores.append(
-                [
-                    dot_t(qs, kv[0, s, :, column]),
-                    dot_t(qs, kv_pair[0, s, :, column]),
-                    jnp.where(block_live, dot_t(qs, block[0, s, :, column]), -1e30),
-                ]
-            )
+        for qs, s, own in zip(asked, which, own_scores):
+            extra = jnp.where(block_live, dot_t(qs, block[0, s, :, column]), -1e30)
+            scores.append([own, dot_t(qs, kv_pair[0, s, :, column]), extra])
         peaks = []
         for own, other, extra in scores:
             widest = extra

time: 81.5 us -> 82.2 us (level)
  no operation moved by 1% of the time
where the time goes in v6:
time: 82.2 us; the launch traced here: 82.1 us
  Pallas kernels  80.6 us (98%)
  local copies, waits for them, and re-layouts  1.47 us (2%)
    pallas_call x1, Pallas kernels, body(): pl.pallas_call(functools.partial(layer_kernel, dims), out_shape=jax.Shape...  80.6 us

profile of v6, /device:TPU:1, one launch (start us, length us, event | category | flops | bytes accessed | tf_op | source)
XLA Modules:
  0.0 82.1 jit_solution(14192270702823307634)
XLA Ops:
  0.0 80.6 %shard_map.100 = bf16[128,256]{1,0:T(8,128)(2,1)} custom-call(bf16[128,4096]{1,0:T(8,128)(2,1)} %q_hbm.1, bf16[2,4,256,512]{3,2,1,0:T(8,128)(2,1)} %cache_hbm.1, bf16[2,4,2,512]{3,2,1,0:T(2,128)(2,1)} %block_hbm.1, bf16[128,4096]{1,0:T(8,128)(2,1)} %stream_hbm.1, bf16[256,4096]{1,0:T(8,128)(2,1)} %proj_hbm.1, f32[1,4096]{1,0:T(1,128)} %bitcast.3, ...), custom_call_target="tpu_custom_call" | custom-call | tf_op jit(solution)/shard_map/pallas_call | solution.py:721
  80.6 1.5 %copy.12 = bf16[128,256]{1,0:T(8,128)(2,1)} copy(bf16[128,256]{1,0:T(8,128)(2,1)} %shard_map.100) | data formatting | bytes 131072
